TPU v7x, 128 devices: a whole 4x4x4 slice. The times are simulated.
128 devices in a mesh: gx: 16 (over z, y), gy: 8 (over x, core).
Axes of the slice: x: 4, y: 4, z: 4, core: 2. Of those that a mesh axis runs over, the one named last changes fastest.
Arguments:
- field: float32 [256, 1024, 512], P('gx', 'gy'), may hold values from -6144 to 6144
- conduct: float32 [256, 1024, 512], P('gx', 'gy'), may hold values from 0.2 to 4
- seg_cell: int32 [128, 128, 4], P(('gx', 'gy')), may hold values from 0 to 1048575
- seg_count: int32 [128, 128], P(('gx', 'gy')), may hold values from 1 to 4, as said below
- currents: float32 [128, 128, 4], P(('gx', 'gy')), may hold values from -6 to 6
- coupling: bfloat16 [128, 512, 512], P(('gx', 'gy')), may hold values from -0.0048828125 to 0.0048828125
Outputs:
- field_next: float32 [256, 1024, 512], P('gx', 'gy')
- currents_next: float32 [128, 128, 4], P(('gx', 'gy'))
Inputs may be any that keep to these rules, and one draw needn't show every extreme that they name: `seg_cell`: A flat cell index within the sending device's block. `seg_count`: every count is 1 to 4; for one owner drawn from the seed every sender's count is 4.
All inputs are finite; a program needn't handle non-finite values.
Results may differ from a plain program's by a relative error of at most 0.002.
Values sent between devices are 32-bit elements; how exact they have to be, the bound alone decides.
A program may use at most 256 MiB of HBM per device.

v0:
```python
import functools

import jax
import jax.numpy as jnp
from jax import lax
from jax.experimental import pallas as pl
from jax.experimental.pallas import tpu as pltpu
from jax.sharding import PartitionSpec as P

MESH = pl.DeviceIdType.MESH
F32 = jnp.float32
BF16 = jnp.bfloat16

CX, CY, NZ, CAP = 16, 128, 512, 4
GX, GY = 16, 8
WIRE = 512
KX = 8.0 * CX * CX
KY = 8.0 * CY * CY
INJECT = 4.0 * KY**0.5
PLANE = CY * CX


def inverse(value):
    return 1.0 / value


def split3(value):
    high = value.astype(BF16).astype(F32)
    rest = value - high
    middle = rest.astype(BF16).astype(F32)
    return high, middle, rest - middle


def kernel(
    field,
    conduct,
    cell_s,
    cell_v,
    count_v,
    cur_v,
    coupling,
    out,
    cur_out,
    fb,
    cb,
    mx,
    ax,
    xs,
    xr,
    xw,
    vs,
    vr,
    ht,
    my,
    ay,
    cw,
    hot,
    bh,
    bl,
    samp,
    zcol,
    p1s,
    p1r,
    p2s,
    p2r,
    ys,
    ga,
    gat,
    gb,
    ycs,
    ycr,
    yrs,
    yrr,
    yvs,
    yvr,
    fsem,
    csem,
    wsem,
    xsem,
    vsem,
    s1,
    s2,
    sa,
    sb,
    syc,
    syr,
    syv,
    osem,
):
    me_x = lax.axis_index("gx")
    me_y = lax.axis_index("gy")

    def peer_x(step):
        return lax.rem(me_x + step, GX)

    def peer_y(step):
        return lax.rem(me_y + step, GY)

    def chunk(d):
        return pl.ds(pl.multiple_of(d * 8, 8), 8)

    def quarter(q):
        return slice(128 * q, 128 * q + 128)

    def in_copies(d):
        copies = []
        for q in range(4):
            for src, dst, sem in ((conduct, cb, csem), (field, fb, fsem)):
                copies.append(
                    pltpu.make_async_copy(
                        src.at[:, chunk(d), quarter(q)], dst.at[q, :, chunk(d), :], sem.at[d, q]
                    )
                )
        return copies

    def load4(ref, x, rows):
        return jnp.concatenate([ref[q, x, rows, :] for q in range(4)], axis=1)

    def order(t):
        u = 15 - t
        return lax.rem(me_x // 4 + u // 4, 4) * 4 + lax.rem(me_x + lax.rem(u, 4), 4)

    def start_in(t, carry):
        for copy in in_copies(order(t)):
            copy.start()
        return carry

    lax.fori_loop(0, GX, start_in, 0)
    weights = pltpu.make_async_copy(coupling, cw, wsem)
    weights.start()

    barrier = pltpu.get_barrier_semaphore()

    def greet_x(t, carry):
        pl.semaphore_signal(barrier, inc=1, device_id=(peer_x(t), me_y), device_id_type=MESH)
        return carry

    def greet_y(t, carry):
        pl.semaphore_signal(barrier, inc=1, device_id=(me_x, peer_y(t)), device_id_type=MESH)
        return carry

    lax.fori_loop(1, GX, greet_x, 0)
    lax.fori_loop(1, GY, greet_y, 0)
    pl.semaphore_wait(barrier, GX - 1 + GY - 1)

    def copy_x(src, dst, sems, slot, to, who):
        return pltpu.make_async_remote_copy(
            src_ref=src, dst_ref=dst, send_sem=sems.at[0, slot], recv_sem=sems.at[1, who],
            device_id=(to, me_y), device_id_type=MESH,
        )

    def copy_y(src, dst, sems, slot, to, who):
        return pltpu.make_async_remote_copy(
            src_ref=src, dst_ref=dst, send_sem=sems.at[0, slot], recv_sem=sems.at[1, who],
            device_id=(me_x, to), device_id_type=MESH,
        )

    def each(count, body, start=1):
        def run(t, carry):
            body(t)
            return carry

        lax.fori_loop(start, count, run, 0)

    lane_z = lax.broadcasted_iota(jnp.int32, (8, NZ), 1)
    scale_f = 1.0 / (KX * KY)

    def eliminate(t, carry):
        d = order(t)
        for copy in in_copies(d):
            copy.wait()
        rows = chunk(d)

        def ground(x):
            return (1.0 / KX) + (0.5 / KX) * load4(cb, x, rows)

        def source(x):
            value = load4(fb, x, rows)
            up = jnp.where(lane_z == NZ - 1, 0.0, pltpu.roll(value, NZ - 1, 1))
            down = jnp.where(lane_z == 0, 0.0, pltpu.roll(value, 1, 1))
            return (0.5 * scale_f) * value + (0.25 * scale_f) * (up + down)

        a = jnp.ones((8, NZ), F32)
        g = ground(0)
        f = source(0)
        gp = jnp.zeros((8, NZ), F32)
        fp = jnp.zeros((8, NZ), F32)
        for x in range(CX - 1):
            m = inverse(a + g + 1.0)
            am = a * m
            b = f * m
            mx[x, rows, :] = m
            ax[x, rows, :] = am
            gp = gp + am * g
            fp = fp + am * f
            f = source(x + 1) + b
            for q in range(4):
                fb[q, x, rows, :] = b[:, quarter(q)]
            g = ground(x + 1) + g * m
            a = am
        for slot, value in enumerate((a, g, f, gp, fp)):
            xs[d, slot] = value

        @pl.when(t < GX - 1)
        def _():
            copy_x(xs.at[d], xr.at[me_x], xsem, d, d, me_x).start()

        return carry

    lax.fori_loop(0, GX, eliminate, 0)
    xr[me_x] = xs[me_x]

    cb2 = cb.reshape(4 * PLANE, 128)

    def ground_y(y):
        return [(1.0 / KY) + (0.5 / KY) * cb2[pl.ds(q * PLANE + y, CX, stride=CY), :] for q in range(4)]

    def at_y(y, q):
        return pl.ds(pl.multiple_of(q * PLANE + y * CX, CX), CX)

    def factor(y, state):
        a, g, gp = state
        after = ground_y(y + 1)
        a_new, g_new, gp_new = [], [], []
        for q in range(4):
            m = inverse(a[q] + g[q] + 1.0)
            am = a[q] * m
            my[at_y(y, q), :] = m
            ay[at_y(y, q), :] = am
            gp_new.append(gp[q] + am * g[q])
            g_new.append(after[q] + g[q] * m)
            a_new.append(am)
        return a_new, g_new, gp_new

    ones = [jnp.ones((CX, 128), F32) for _ in range(4)]
    zeros = [jnp.zeros((CX, 128), F32) for _ in range(4)]
    a_y, g_y, gp_y = lax.fori_loop(0, CY - 1, factor, (ones, ground_y(0), zeros))
    for q in range(4):
        for h in range(2):
            for slot, value in enumerate((a_y, g_y, gp_y)):
                ycs[2 * q + h, slot] = value[q][8 * h : 8 * h + 8]

    def send_yc(t):
        to = peer_y(t)
        copy_y(ycs.at[to], ycr.at[me_y], syc, to, to, me_y).start()

    each(GY, send_yc)
    ycr[me_y] = ycs[me_y]

    cells = cell_v[...]
    slot_of = lax.broadcasted_iota(jnp.int32, (CAP, 128), 0)
    filled = slot_of < count_v[...]
    place_z = jnp.where(filled, cells & (NZ - 1), -1)
    place_r = ((cells >> 9) & (CY - 1)) * CX + (cells >> 16)
    zcol[...] = jnp.concatenate([place_z, jnp.full((128 - CAP, 128), -1, jnp.int32)], axis=0).T

    def build_hot(n, carry):
        base = n * 128
        rows = lax.broadcasted_iota(jnp.int32, (128, 128), 0) + base
        for k in range(CAP):
            match = jnp.where(rows == place_r[k : k + 1, :], 1.0, 0.0)
            hot[pl.ds(pl.multiple_of(base, 128), 128), 128 * k : 128 * k + 128] = match.astype(BF16)
        return carry

    lax.fori_loop(0, PLANE // 128, build_hot, 0)

    row_m = lax.broadcasted_iota(jnp.int32, (128, WIRE), 0)
    lane_m = lax.broadcasted_iota(jnp.int32, (128, WIRE), 1)
    spread = [jnp.where(lane_m == row_m * CAP + k, 1.0, 0.0).astype(BF16) for k in range(CAP)]

    def three_rows(row):
        high, middle, low = split3(row)
        index = lax.broadcasted_iota(jnp.int32, (16, row.shape[1]), 0)
        stack = jnp.where(index == 0, high, jnp.where(index == 1, middle, jnp.where(index == 2, low, 0.0)))
        return stack.astype(BF16)

    def exact_dot(row, matrix, dims):
        product = lax.dot_general(three_rows(row), matrix, (dims, ((), ())), preferred_element_type=F32)
        return (product[2:3] + product[1:2]) + product[0:1]

    cur_row = jnp.zeros((1, WIRE), F32)
    for k in range(CAP):
        cur_row = cur_row + exact_dot(cur_v[k : k + 1, :], spread[k], ((1,), (0,)))
    p2s[...] = jnp.zeros_like(p2s)
    ys[...] = jnp.zeros_like(ys)

    def arrive_x(t):
        frm = peer_x(t)
        copy_x(xs.at[frm], xr.at[frm], xsem, frm, frm, frm).wait_recv()

    each(GX, arrive_x)

    def forward_x(r, state):
        q, phi = state
        more_g = jnp.where(r < GX - 1, xr[jnp.minimum(r + 1, GX - 1), 3], 1.0)
        more_f = jnp.where(r < GX - 1, xr[jnp.minimum(r + 1, GX - 1), 4], 0.0)
        a = xr[r, 0]
        m = inverse(a + q)
        am = jnp.where(r == 0, 0.0, a * m)
        q_new = xr[r, 1] + more_g + jnp.where(r == 0, a, am * q)
        phi_new = xr[r, 2] + more_f + am * phi
        xw[r, 0] = am
        xw[r, 1] = m * phi
        return q_new, phi_new

    blank = jnp.zeros((8, NZ), F32)
    q_x, phi_x = lax.fori_loop(0, GX, forward_x, (blank, blank))

    def backward_x(n, value):
        r = GX - 1 - n
        vs[r, 1] = value
        west = xw[r, 1] + xw[r, 0] * value
        west = jnp.where(r == 0, 0.0, west)
        vs[r, 0] = west
        return west

    lax.fori_loop(0, GX, backward_x, phi_x * inverse(q_x))

    def send_v(t):
        to = peer_x(t)
        copy_x(vs.at[to], vr.at[me_x], vsem, to, to, me_x).start()

    each(GX, send_v)
    vr[me_x] = vs[me_x]

    def substitute(t, carry):
        d = peer_x(t)

        @pl.when(t > 0)
        def _():
            copy_x(vs.at[d], vr.at[d], vsem, d, d, d).wait_recv()

        rows = chunk(d)
        west = vr[d, 0]
        value = vr[d, 1]
        for x in range(CX - 1, -1, -1):
            if x < CX - 1:
                value = load4(fb, x, rows) + ax[x, rows, :] * west + mx[x, rows, :] * value
            for q in range(4):
                ht[pl.ds(q * PLANE + d * (8 * CX) + x, 8, stride=CX), :] = value[:, 128 * q : 128 * q + 128]
        return carry

    lax.fori_loop(0, GX, substitute, 0)

    def take(o, carry):
        for k in range(CAP):
            c = cell_s[k, o]
            row = ((c >> 7) & 3) * PLANE + ((c >> 9) & (CY - 1)) * CX + (c >> 16)
            samp[pl.ds(k * 128 + o, 1), :] = ht[pl.ds(row, 1), :]
        return carry

    lax.fori_loop(0, 128, take, 0)

    lanes = lax.broadcasted_iota(jnp.int32, (128, 128), 1)
    mine = lax.rem(me_x, 4) * 32 + me_y * CAP
    placed = jnp.zeros((128, 128), F32)
    for k in range(CAP):
        z = zcol[:, k : k + 1]
        hit = ((z & 127) == lanes) & (z >= 0)
        value = jnp.sum(jnp.where(hit, samp[128 * k : 128 * k + 128, :], 0.0), axis=1, keepdims=True) * KY
        placed = jnp.where(lanes == mine + k, value, placed)
    p1s[...] = placed.reshape(GX, GY, 128)

    def send_1(t):
        to = peer_x(t)
        copy_x(p1s.at[to], p1r.at[me_x], s1, to, to, me_x).start()

    def arrive_1(t):
        frm = peer_x(t)
        copy_x(p1s.at[frm], p1r.at[frm], s1, frm, frm, frm).wait_recv()

    each(GX, send_1)
    p1r[me_x] = p1s[me_x]
    each(GX, arrive_1)
    for a in range(4):
        total = (p1r[4 * a] + p1r[4 * a + 1]) + (p1r[4 * a + 2] + p1r[4 * a + 3])
        for j in range(GY):
            p2s[j, a : a + 1, :] = total[j : j + 1, :]

    def send_2(t):
        to = peer_y(t)
        copy_y(p2s.at[to], p2r.at[me_y], s2, to, to, me_y).start()

    def arrive_2(t):
        frm = peer_y(t)
        copy_y(p2s.at[frm], p2r.at[frm], s2, frm, frm, frm).wait_recv()

    each(GY, send_2)
    p2r[me_y] = p2s[me_y]
    each(GY, arrive_2)
    gathered = p2r[0]
    for j in range(1, GY):
        gathered = gathered + p2r[j]
    row = jnp.concatenate([gathered[a : a + 1, :] for a in range(4)], axis=1)
    weights.wait()
    new_row = 0.5 * cur_row + exact_dot(row, cw[...], ((1,), (1,)))
    for a in range(4):
        ys[a : a + 1, :] = new_row[:, 128 * a : 128 * a + 128]

    def send_a(t):
        to = peer_y(t)
        copy_y(ys, ga.at[me_y], sa, to, to, me_y).start()

    def arrive_a(t):
        frm = peer_y(t)
        copy_y(ys, ga.at[frm], sa, frm, frm, frm).wait_recv()

    each(GY, send_a)
    ga[me_y] = ys[...]
    for k in range(CAP):
        cur_out[k : k + 1, :] = exact_dot(new_row, spread[k], ((1,), (1,)))
    each(GY, arrive_a)
    for j in range(GY):
        part = ga[j]
        for a in range(4):
            gat[a, j : j + 1, :] = part[a : a + 1, :]

    def send_b(t):
        to = peer_x(t)
        copy_x(gat.at[to // 4], gb.at[me_x], sb, to, to, me_x).start()

    def arrive_b(t):
        frm = peer_x(t)
        copy_x(gat.at[0], gb.at[frm], sb, frm, frm, frm).wait_recv()

    each(GX, send_b)
    gb[me_x] = gat[me_x // 4]
    each(GX, arrive_b)

    back = gb[...].reshape(128, 128)
    lane_k = lax.broadcasted_iota(jnp.int32, (128, NZ), 1)
    for k in range(CAP):
        value = jnp.sum(jnp.where(lanes == mine + k, back, 0.0), axis=1, keepdims=True) * (INJECT / KY)
        spot = jnp.where(lane_k == zcol[:, k : k + 1], value, 0.0)
        high = spot.astype(BF16)
        bh[128 * k : 128 * k + 128, :] = high
        bl[128 * k : 128 * k + 128, :] = (spot - high.astype(F32)).astype(BF16)

    def scatter(n, carry):
        rows = pl.ds(pl.multiple_of(n * 256, 256), 256)
        part = hot[rows, :]
        added = jnp.dot(part, bh[...], preferred_element_type=F32) + jnp.dot(part, bl[...], preferred_element_type=F32)
        for q in range(4):
            where = pl.ds(pl.multiple_of(q * PLANE + n * 256, 256), 256)
            ht[where, :] = ht[where, :] + added[:, 128 * q : 128 * q + 128]
        return carry

    lax.fori_loop(0, PLANE // 256, scatter, 0)

    def forward_y(y, state):
        f, fp = state
        f_new, fp_new = [], []
        for q in range(4):
            b = f[q] * my[at_y(y, q), :]
            fp_new.append(fp[q] + ay[at_y(y, q), :] * f[q])
            f_new.append(ht[at_y(y + 1, q), :] + b)
            ht[at_y(y, q), :] = b
        return f_new, fp_new

    first = [ht[at_y(0, q), :] for q in range(4)]
    f_y, fp_y = lax.fori_loop(0, CY - 1, forward_y, (first, zeros))
    for q in range(4):
        for h in range(2):
            for slot, value in enumerate((f_y, fp_y)):
                yrs[2 * q + h, slot] = value[q][8 * h : 8 * h + 8]

    def send_yr(t):
        to = peer_y(t)
        copy_y(yrs.at[to], yrr.at[me_y], syr, to, to, me_y).start()

    def arrive_yr(t):
        frm = peer_y(t)
        copy_y(yrs.at[frm], yrr.at[frm], syr, frm, frm, frm).wait_recv()

    def arrive_yc(t):
        frm = peer_y(t)
        copy_y(ycs.at[frm], ycr.at[frm], syc, frm, frm, frm).wait_recv()

    each(GY, send_yr)
    yrr[me_y] = yrs[me_y]
    each(GY, arrive_yc)
    m_list = [None]
    q_y = ycr[0, 0] + ycr[0, 1] + ycr[1, 2]
    for r in range(1, GY):
        a = ycr[r, 0]
        m = inverse(a + q_y)
        m_list.append((a * m, m))
        more = ycr[r + 1, 2] if r < GY - 1 else 1.0
        q_y = ycr[r, 1] + more + a * m * q_y
    last = inverse(q_y)
    each(GY, arrive_yr)
    phi = yrr[0, 0] + yrr[1, 1]
    phis = [phi]
    for r in range(1, GY):
        more = yrr[r + 1, 1] if r < GY - 1 else 0.0
        phi = yrr[r, 0] + more + m_list[r][0] * phi
        phis.append(phi)
    value = phi * last
    for r in range(GY - 1, 0, -1):
        yvs[r, 1] = value
        value = m_list[r][1] * phis[r - 1] + m_list[r][0] * value
        yvs[r, 0] = value
    yvs[0, 1] = value
    yvs[0, 0] = jnp.zeros((8, 128), F32)

    def send_yv(t):
        to = peer_y(t)
        copy_y(yvs.at[to], yvr.at[me_y], syv, to, to, me_y).start()

    def arrive_yv(t):
        frm = peer_y(t)
        copy_y(yvs.at[frm], yvr.at[frm], syv, frm, frm, frm).wait_recv()

    each(GY, send_yv)
    yvr[me_y] = yvs[me_y]
    each(GY, arrive_yv)

    west_y = [jnp.concatenate([yvr[2 * q, 0], yvr[2 * q + 1, 0]], axis=0) for q in range(4)]
    east_y = [jnp.concatenate([yvr[2 * q, 1], yvr[2 * q + 1, 1]], axis=0) for q in range(4)]
    ob2 = fb.reshape(4 * PLANE, 128)

    def put(y, value):
        for q in range(4):
            ob2[pl.ds(q * PLANE + y, CX, stride=CY), :] = value[q]

    def out_copies(c):
        return [
            pltpu.make_async_copy(fb.at[q, :, chunk(c), :], out.at[:, chunk(c), quarter(q)], osem.at[c, q])
            for q in range(4)
        ]

    def finish(n, value):
        c = CY // 8 - 1 - n
        for back_step in range(8):
            y = c * 8 + 7 - back_step
            new = []
            for q in range(4):
                new.append(ht[at_y(y, q), :] + ay[at_y(y, q), :] * west_y[q] + my[at_y(y, q), :] * value[q])
            value = new
            put(y, value)
        for copy in out_copies(c):
            copy.start()
        return value

    for q in range(4):
        ht[at_y(CY - 1, q), :] = jnp.zeros((CX, 128), F32)
        ay[at_y(CY - 1, q), :] = jnp.zeros((CX, 128), F32)
        my[at_y(CY - 1, q), :] = jnp.ones((CX, 128), F32)
    lax.fori_loop(0, CY // 8, finish, east_y)

    def drain_x(t):
        to = peer_x(t)
        copy_x(xs.at[to], xr.at[me_x], xsem, to, to, me_x).wait_send()
        copy_x(vs.at[to], vr.at[me_x], vsem, to, to, me_x).wait_send()
        copy_x(p1s.at[to], p1r.at[me_x], s1, to, to, me_x).wait_send()
        copy_x(gat.at[0], gb.at[me_x], sb, to, to, me_x).wait_send()

    def drain_y(t):
        to = peer_y(t)
        copy_y(p2s.at[to], p2r.at[me_y], s2, to, to, me_y).wait_send()
        copy_y(ys, ga.at[me_y], sa, to, to, me_y).wait_send()
        copy_y(ycs.at[to], ycr.at[me_y], syc, to, to, me_y).wait_send()
        copy_y(yrs.at[to], yrr.at[me_y], syr, to, to, me_y).wait_send()
        copy_y(yvs.at[to], yvr.at[me_y], syv, to, to, me_y).wait_send()

    each(GX, drain_x)
    each(GY, drain_y)

    def drain_out(c):
        for copy in out_copies(c):
            copy.wait()

    each(CY // 8, drain_out, 0)


def local(field, conduct, seg_cell, seg_count, currents, coupling):
    hbm = pl.BlockSpec(memory_space=pltpu.HBM)
    vmem = pl.BlockSpec(memory_space=pltpu.VMEM)
    smem = pl.BlockSpec(memory_space=pltpu.SMEM)
    cells = seg_cell[0].T
    block = lambda *shape: pltpu.VMEM(shape, F32)
    sems = lambda count: pltpu.SemaphoreType.DMA((2, count))
    scratch = [
        block(4, CX, CY, 128),
        block(4, CX, CY, 128),
        block(CX - 1, CY, NZ),
        block(CX - 1, CY, NZ),
        block(GX, 5, 8, NZ),
        block(GX, 5, 8, NZ),
        block(GX, 2, 8, NZ),
        block(GX, 2, 8, NZ),
        block(GX, 2, 8, NZ),
        block(4 * PLANE, 128),
        block(4 * PLANE, 128),
        block(4 * PLANE, 128),
        pltpu.VMEM((WIRE, WIRE), BF16),
        pltpu.VMEM((PLANE, WIRE), BF16),
        pltpu.VMEM((WIRE, NZ), BF16),
        pltpu.VMEM((WIRE, NZ), BF16),
        block(WIRE, 128),
        pltpu.VMEM((128, 128), jnp.int32),
        block(GX, 8, 128),
        block(GX, 8, 128),
        block(GY, 8, 128),
        block(GY, 8, 128),
        block(8, 128),
        block(GY, 8, 128),
        block(4, 8, 128),
        block(GX, 8, 128),
        block(GY, 3, 8, 128),
        block(GY, 3, 8, 128),
        block(GY, 2, 8, 128),
        block(GY, 2, 8, 128),
        block(GY, 2, 8, 128),
        block(GY, 2, 8, 128),
        pltpu.SemaphoreType.DMA((GX, 4)),
        pltpu.SemaphoreType.DMA((GX, 4)),
        pltpu.SemaphoreType.DMA,
        sems(GX),
        sems(GX),
        sems(GX),
        sems(GY),
        sems(GY),
        sems(GX),
        sems(GY),
        sems(GY),
        sems(GY),
        pltpu.SemaphoreType.DMA((CY // 8, 4)),
    ]
    field_next, currents_next = pl.pallas_call(
        kernel,
        out_shape=(
            jax.ShapeDtypeStruct((CX, CY, NZ), F32),
            jax.ShapeDtypeStruct((CAP, 128), F32),
        ),
        in_specs=[hbm, hbm, smem, vmem, vmem, vmem, hbm],
        out_specs=(hbm, vmem),
        scratch_shapes=scratch,
        compiler_params=pltpu.CompilerParams(
            collective_id=0, has_side_effects=True, vmem_limit_bytes=56 * 1024 * 1024
        ),
    )(field, conduct, cells, cells, seg_count, currents[0].T, coupling[0])
    return field_next, currents_next.T[None]


def solution(mesh):
    placed = (
        P("gx", "gy", None),
        P("gx", "gy", None),
        P(("gx", "gy"), None, None),
        P(("gx", "gy"), None),
        P(("gx", "gy"), None, None),
        P(("gx", "gy"), None, None),
    )
    return jax.shard_map(
        local,
        mesh=mesh,
        in_specs=placed,
        out_specs=(P("gx", "gy", None), P(("gx", "gy"), None, None)),
        check_vma=False,
    )
```

profile of v0, /device:TPU:1, one launch (start us, length us, event | category | flops | bytes accessed | tf_op | source)
XLA Modules:
  0.0 86.4 jit_solution(4726099479441566178)
XLA Ops:
  0.6 80.4 %shard_map.77 = (f32[16,128,512]{2,1,0:T(8,128)}, f32[4,128]{1,0:T(4,128)}) custom-call(f32[16,128,512]{2,1,0:T(8,128)} %field.1, f32[16,128,512]{2,1,0:T(8,128)} %conduct.1, s32[4,128]{1,0:T(4,128)} %bitcast.11, s32[4,128]{1,0:T(4,128)} %bitcast.12, s32[1,128]{1,0:T(1,128)} %count_v.1, f32[4,128]{1,0:T(4,128)} %bitcast.13, bf16[512,512]{1,0:T(8,128)(2,1)} %bitcast.10), custom_call_target="tpu_custom_call" | custom-call | tf_op jit(solution)/shard_map/pallas_call | solution.py:630
  81.0 0.0 copy-start
  81.0 4.8 %copy.10 = f32[16,128,512]{2,1,0:T(8,128)} copy(f32[16,128,512]{2,1,0:T(8,128)} %get-tuple-element.8) | data formatting | bytes 8388608
  85.8 0.0 copy-done
  85.8 0.6 copy.11
Async XLA Ops:
  81.0 4.8 %copy-start = (f32[4,128]{1,0:T(4,128)S(1)}, f32[4,128]{1,0:T(4,128)}, u32[]{:S(2)}) copy-start(f32[4,128]{1,0:T(4,128)} %get-tuple-element.5) | copy-start | bytes 6148
where the time goes:
time: 86.6 us; the launch traced here: 86.4 us
  Pallas kernels  80.4 us (93%)
  local copies, waits for them, and re-layouts  5.39 us (6%)
    pallas_call x1, Pallas kernels, local(): pl.pallas_call(kernel, out_shape=(jax.ShapeDtypeStruct((CX, CY, NZ), F32)...  80.4 us
    unnamed x4, local copies, waits for them, and re-layouts  5.39 us

commit v1 on v0

--- a/solution.py
+++ b/solution.py
@@ -18,10 +18,12 @@
 KY = 8.0 * CY * CY
 INJECT = 4.0 * KY**0.5
 PLANE = CY * CX
+UNITS = 8
+EARLY = 8
 
 
 def inverse(value):
-    return 1.0 / value
+    return pl.reciprocal(value, approx=True)
 
 
 def split3(value):
@@ -39,7 +41,7 @@
     count_v,
     cur_v,
     coupling,
-    out,
+    ob,
     cur_out,
     fb,
     cb,
@@ -47,7 +49,6 @@
     ax,
     xs,
     xr,
-    xw,
     vs,
     vr,
     ht,
@@ -59,6 +60,7 @@
     bl,
     samp,
     zcol,
+    rows_s,
     p1s,
     p1r,
     p2s,
@@ -85,7 +87,6 @@
     syc,
     syr,
     syv,
-    osem,
 ):
     me_x = lax.axis_index("gx")
     me_y = lax.axis_index("gy")
@@ -95,6 +96,13 @@
 
     def peer_y(step):
         return lax.rem(me_y + step, GY)
+
+    def each(count, body, start=1):
+        def run(t, carry):
+            body(t)
+            return carry
+
+        lax.fori_loop(start, count, run, 0)
 
     def chunk(d):
         return pl.ds(pl.multiple_of(d * 8, 8), 8)
@@ -107,14 +115,12 @@
         for q in range(4):
             for src, dst, sem in ((conduct, cb, csem), (field, fb, fsem)):
                 copies.append(
-                    pltpu.make_async_copy(
-                        src.at[:, chunk(d), quarter(q)], dst.at[q, :, chunk(d), :], sem.at[d, q]
-                    )
+                    pltpu.make_async_copy(src.at[:, chunk(d), quarter(q)], dst.at[q, d], sem.at[d, q])
                 )
         return copies
 
-    def load4(ref, x, rows):
-        return jnp.concatenate([ref[q, x, rows, :] for q in range(4)], axis=1)
+    def load4(ref, d, x):
+        return jnp.concatenate([ref[q, d, x] for q in range(4)], axis=1)
 
     def order(t):
         u = 15 - t
@@ -141,8 +147,6 @@
 
     lax.fori_loop(1, GX, greet_x, 0)
     lax.fori_loop(1, GY, greet_y, 0)
-    pl.semaphore_wait(barrier, GX - 1 + GY - 1)
-
     def copy_x(src, dst, sems, slot, to, who):
         return pltpu.make_async_remote_copy(
             src_ref=src, dst_ref=dst, send_sem=sems.at[0, slot], recv_sem=sems.at[1, who],
@@ -155,27 +159,18 @@
             device_id=(me_x, to), device_id_type=MESH,
         )
 
-    def each(count, body, start=1):
-        def run(t, carry):
-            body(t)
-            return carry
-
-        lax.fori_loop(start, count, run, 0)
-
     lane_z = lax.broadcasted_iota(jnp.int32, (8, NZ), 1)
     scale_f = 1.0 / (KX * KY)
 
-    def eliminate(t, carry):
-        d = order(t)
+    def eliminate(d):
         for copy in in_copies(d):
             copy.wait()
-        rows = chunk(d)
 
         def ground(x):
-            return (1.0 / KX) + (0.5 / KX) * load4(cb, x, rows)
+            return (1.0 / KX) + (0.5 / KX) * load4(cb, d, x)
 
         def source(x):
-            value = load4(fb, x, rows)
+            value = load4(fb, d, x)
             up = jnp.where(lane_z == NZ - 1, 0.0, pltpu.roll(value, NZ - 1, 1))
             down = jnp.where(lane_z == 0, 0.0, pltpu.roll(value, 1, 1))
             return (0.5 * scale_f) * value + (0.25 * scale_f) * (up + down)
@@ -189,56 +184,70 @@
             m = inverse(a + g + 1.0)
             am = a * m
             b = f * m
-            mx[x, rows, :] = m
-            ax[x, rows, :] = am
             gp = gp + am * g
             fp = fp + am * f
             f = source(x + 1) + b
             for q in range(4):
-                fb[q, x, rows, :] = b[:, quarter(q)]
+                mx[q, d, x] = m[:, quarter(q)]
+                ax[q, d, x] = am[:, quarter(q)]
+                fb[q, d, x] = b[:, quarter(q)]
             g = ground(x + 1) + g * m
             a = am
         for slot, value in enumerate((a, g, f, gp, fp)):
-            xs[d, slot] = value
+            for q in range(4):
+                xs[q, d, slot] = value[:, quarter(q)]
+
+    def send_x(q, d):
+        copy_x(xs.at[q, d], xr.at[q, me_x], xsem.at[q], d, d, me_x).start()
+
+    def eliminate_and_send(t):
+        d = order(t)
+        eliminate(d)
 
         @pl.when(t < GX - 1)
         def _():
-            copy_x(xs.at[d], xr.at[me_x], xsem, d, d, me_x).start()
-
-        return carry
-
-    lax.fori_loop(0, GX, eliminate, 0)
-    xr[me_x] = xs[me_x]
+            send_x(0, d)
+
+    each(EARLY, lambda t: eliminate(order(t)), 0)
+    pl.semaphore_wait(barrier, GX - 1 + GY - 1)
+    each(EARLY, lambda t: send_x(0, order(t)), 0)
+    each(GX, eliminate_and_send, EARLY)
+    for q in range(1, 4):
+        each(GX - 1, lambda t, q=q: send_x(q, order(t)), 0)
+    for q in range(4):
+        xr[q, me_x] = xs[q, me_x]
 
     cb2 = cb.reshape(4 * PLANE, 128)
 
+    def spread_rows(y, u):
+        return pl.ds((u // 2) * PLANE + (y // 8) * (8 * CX) + (u % 2) * 64 + lax.rem(y, 8), 8, stride=8)
+
     def ground_y(y):
-        return [(1.0 / KY) + (0.5 / KY) * cb2[pl.ds(q * PLANE + y, CX, stride=CY), :] for q in range(4)]
-
-    def at_y(y, q):
-        return pl.ds(pl.multiple_of(q * PLANE + y * CX, CX), CX)
+        return [(1.0 / KY) + (0.5 / KY) * cb2[spread_rows(y, u), :] for u in range(UNITS)]
+
+    def at_y(y, u):
+        return pl.ds(pl.multiple_of(u * (8 * CY) + y * 8, 8), 8)
 
     def factor(y, state):
         a, g, gp = state
         after = ground_y(y + 1)
         a_new, g_new, gp_new = [], [], []
-        for q in range(4):
-            m = inverse(a[q] + g[q] + 1.0)
-            am = a[q] * m
-            my[at_y(y, q), :] = m
-            ay[at_y(y, q), :] = am
-            gp_new.append(gp[q] + am * g[q])
-            g_new.append(after[q] + g[q] * m)
+        for u in range(UNITS):
+            m = inverse(a[u] + g[u] + 1.0)
+            am = a[u] * m
+            my[at_y(y, u), :] = m
+            ay[at_y(y, u), :] = am
+            gp_new.append(gp[u] + am * g[u])
+            g_new.append(after[u] + g[u] * m)
             a_new.append(am)
         return a_new, g_new, gp_new
 
-    ones = [jnp.ones((CX, 128), F32) for _ in range(4)]
-    zeros = [jnp.zeros((CX, 128), F32) for _ in range(4)]
+    ones = [jnp.ones((8, 128), F32) for _ in range(UNITS)]
+    zeros = [jnp.zeros((8, 128), F32) for _ in range(UNITS)]
     a_y, g_y, gp_y = lax.fori_loop(0, CY - 1, factor, (ones, ground_y(0), zeros))
-    for q in range(4):
-        for h in range(2):
-            for slot, value in enumerate((a_y, g_y, gp_y)):
-                ycs[2 * q + h, slot] = value[q][8 * h : 8 * h + 8]
+    for u in range(UNITS):
+        for slot, value in enumerate((a_y, g_y, gp_y)):
+            ycs[u, slot] = value[u]
 
     def send_yc(t):
         to = peer_y(t)
@@ -251,8 +260,16 @@
     slot_of = lax.broadcasted_iota(jnp.int32, (CAP, 128), 0)
     filled = slot_of < count_v[...]
     place_z = jnp.where(filled, cells & (NZ - 1), -1)
-    place_r = ((cells >> 9) & (CY - 1)) * CX + (cells >> 16)
+    place_r = (cells >> 19) * (8 * CY) + ((cells >> 9) & (CY - 1)) * 8 + ((cells >> 16) & 7)
     zcol[...] = jnp.concatenate([place_z, jnp.full((128 - CAP, 128), -1, jnp.int32)], axis=0).T
+
+    def find(o):
+        for k in range(CAP):
+            c = cell_s[k, o]
+            row = ((c >> 7) & 3) * PLANE + (c >> 19) * (8 * CY) + ((c >> 9) & (CY - 1)) * 8 + ((c >> 16) & 7)
+            rows_s[k * 128 + o] = row
+
+    each(128, find, 0)
 
     def build_hot(n, carry):
         base = n * 128
@@ -284,72 +301,71 @@
     p2s[...] = jnp.zeros_like(p2s)
     ys[...] = jnp.zeros_like(ys)
 
-    def arrive_x(t):
-        frm = peer_x(t)
-        copy_x(xs.at[frm], xr.at[frm], xsem, frm, frm, frm).wait_recv()
-
-    each(GX, arrive_x)
-
-    def forward_x(r, state):
-        q, phi = state
-        more_g = jnp.where(r < GX - 1, xr[jnp.minimum(r + 1, GX - 1), 3], 1.0)
-        more_f = jnp.where(r < GX - 1, xr[jnp.minimum(r + 1, GX - 1), 4], 0.0)
-        a = xr[r, 0]
-        m = inverse(a + q)
-        am = jnp.where(r == 0, 0.0, a * m)
-        q_new = xr[r, 1] + more_g + jnp.where(r == 0, a, am * q)
-        phi_new = xr[r, 2] + more_f + am * phi
-        xw[r, 0] = am
-        xw[r, 1] = m * phi
-        return q_new, phi_new
-
-    blank = jnp.zeros((8, NZ), F32)
-    q_x, phi_x = lax.fori_loop(0, GX, forward_x, (blank, blank))
-
-    def backward_x(n, value):
-        r = GX - 1 - n
-        vs[r, 1] = value
-        west = xw[r, 1] + xw[r, 0] * value
-        west = jnp.where(r == 0, 0.0, west)
-        vs[r, 0] = west
-        return west
-
-    lax.fori_loop(0, GX, backward_x, phi_x * inverse(q_x))
-
-    def send_v(t):
-        to = peer_x(t)
-        copy_x(vs.at[to], vr.at[me_x], vsem, to, to, me_x).start()
-
-    each(GX, send_v)
-    vr[me_x] = vs[me_x]
-
-    def substitute(t, carry):
-        d = peer_x(t)
-
-        @pl.when(t > 0)
-        def _():
-            copy_x(vs.at[d], vr.at[d], vsem, d, d, d).wait_recv()
-
-        rows = chunk(d)
-        west = vr[d, 0]
-        value = vr[d, 1]
-        for x in range(CX - 1, -1, -1):
-            if x < CX - 1:
-                value = load4(fb, x, rows) + ax[x, rows, :] * west + mx[x, rows, :] * value
-            for q in range(4):
-                ht[pl.ds(q * PLANE + d * (8 * CX) + x, 8, stride=CX), :] = value[:, 128 * q : 128 * q + 128]
-        return carry
-
-    lax.fori_loop(0, GX, substitute, 0)
-
-    def take(o, carry):
-        for k in range(CAP):
-            c = cell_s[k, o]
-            row = ((c >> 7) & 3) * PLANE + ((c >> 9) & (CY - 1)) * CX + (c >> 16)
-            samp[pl.ds(k * 128 + o, 1), :] = ht[pl.ds(row, 1), :]
-        return carry
-
-    lax.fori_loop(0, 128, take, 0)
+    blank = jnp.zeros((8, 128), F32)
+
+    def reduce_x(q):
+        def arrive(t):
+            frm = peer_x(t)
+            copy_x(xs.at[q, frm], xr.at[q, frm], xsem.at[q], frm, frm, frm).wait_recv()
+
+        each(GX, arrive)
+        q_x = xr[q, 0, 0] + xr[q, 0, 1] + xr[q, 1, 3]
+        phi = xr[q, 0, 2] + xr[q, 1, 4]
+        kept = [None]
+        for r in range(1, GX):
+            a = xr[q, r, 0]
+            m = inverse(a + q_x)
+            am = a * m
+            kept.append((am, m * phi))
+            more_g, more_f = (xr[q, r + 1, 3], xr[q, r + 1, 4]) if r < GX - 1 else (1.0, 0.0)
+            q_x = xr[q, r, 1] + more_g + am * q_x
+            phi = xr[q, r, 2] + more_f + am * phi
+        value = phi * inverse(q_x)
+        for r in range(GX - 1, 0, -1):
+            vs[q, r, 1] = value
+            value = kept[r][1] + kept[r][0] * value
+            vs[q, r, 0] = value
+        vs[q, 0, 1] = value
+        vs[q, 0, 0] = blank
+
+        def send(t):
+            to = peer_x(t)
+            copy_x(vs.at[q, to], vr.at[q, me_x], vsem.at[q], to, to, me_x).start()
+
+        each(GX, send)
+        vr[q, me_x] = vs[q, me_x]
+
+    for q in range(4):
+        reduce_x(q)
+
+    def substitute(q):
+        def arrive(t):
+            frm = peer_x(t)
+            copy_x(vs.at[q, frm], vr.at[q, frm], vsem.at[q], frm, frm, frm).wait_recv()
+
+        def group(n):
+            ds = [n * 4 + i for i in range(4)]
+            west = [vr[q, d, 0] for d in ds]
+            value = [vr[q, d, 1] for d in ds]
+            for x in range(CX - 1, -1, -1):
+                if x < CX - 1:
+                    value = [
+                        (fb[q, d, x] + ax[q, d, x] * west[i]) + mx[q, d, x] * value[i] for i, d in enumerate(ds)
+                    ]
+                for i, d in enumerate(ds):
+                    ht[pl.ds((2 * q + x // 8) * (8 * CY) + d * 64 + x % 8, 8, stride=8), :] = value[i]
+
+        each(GX, arrive)
+        each(4, group, 0)
+
+    for q in range(4):
+        substitute(q)
+
+    def take(n):
+        for i in range(16):
+            samp[pl.ds(n * 16 + i, 1), :] = ht[pl.ds(rows_s[n * 16 + i], 1), :]
+
+    each(WIRE // 16, take, 0)
 
     lanes = lax.broadcasted_iota(jnp.int32, (128, 128), 1)
     mine = lax.rem(me_x, 4) * 32 + me_y * CAP
@@ -450,19 +466,18 @@
     def forward_y(y, state):
         f, fp = state
         f_new, fp_new = [], []
-        for q in range(4):
-            b = f[q] * my[at_y(y, q), :]
-            fp_new.append(fp[q] + ay[at_y(y, q), :] * f[q])
-            f_new.append(ht[at_y(y + 1, q), :] + b)
-            ht[at_y(y, q), :] = b
+        for u in range(UNITS):
+            b = f[u] * my[at_y(y, u), :]
+            fp_new.append(fp[u] + ay[at_y(y, u), :] * f[u])
+            f_new.append(ht[at_y(y + 1, u), :] + b)
+            ht[at_y(y, u), :] = b
         return f_new, fp_new
 
-    first = [ht[at_y(0, q), :] for q in range(4)]
+    first = [ht[at_y(0, u), :] for u in range(UNITS)]
     f_y, fp_y = lax.fori_loop(0, CY - 1, forward_y, (first, zeros))
-    for q in range(4):
-        for h in range(2):
-            for slot, value in enumerate((f_y, fp_y)):
-                yrs[2 * q + h, slot] = value[q][8 * h : 8 * h + 8]
+    for u in range(UNITS):
+        for slot, value in enumerate((f_y, fp_y)):
+            yrs[u, slot] = value[u]
 
     def send_yr(t):
         to = peer_y(t)
@@ -515,43 +530,33 @@
     yvr[me_y] = yvs[me_y]
     each(GY, arrive_yv)
 
-    west_y = [jnp.concatenate([yvr[2 * q, 0], yvr[2 * q + 1, 0]], axis=0) for q in range(4)]
-    east_y = [jnp.concatenate([yvr[2 * q, 1], yvr[2 * q + 1, 1]], axis=0) for q in range(4)]
-    ob2 = fb.reshape(4 * PLANE, 128)
-
-    def put(y, value):
-        for q in range(4):
-            ob2[pl.ds(q * PLANE + y, CX, stride=CY), :] = value[q]
-
-    def out_copies(c):
-        return [
-            pltpu.make_async_copy(fb.at[q, :, chunk(c), :], out.at[:, chunk(c), quarter(q)], osem.at[c, q])
-            for q in range(4)
-        ]
+    west_y = [yvr[u, 0] for u in range(UNITS)]
+    east_y = [yvr[u, 1] for u in range(UNITS)]
+    ob2 = ob.reshape(4 * PLANE, 128)
 
     def finish(n, value):
         c = CY // 8 - 1 - n
         for back_step in range(8):
             y = c * 8 + 7 - back_step
-            new = []
-            for q in range(4):
-                new.append(ht[at_y(y, q), :] + ay[at_y(y, q), :] * west_y[q] + my[at_y(y, q), :] * value[q])
-            value = new
-            put(y, value)
-        for copy in out_copies(c):
-            copy.start()
+            value = [
+                (ht[at_y(y, u), :] + ay[at_y(y, u), :] * west_y[u]) + my[at_y(y, u), :] * value[u]
+                for u in range(UNITS)
+            ]
+            for u in range(UNITS):
+                ob2[spread_rows(y, u), :] = value[u]
         return value
 
-    for q in range(4):
-        ht[at_y(CY - 1, q), :] = jnp.zeros((CX, 128), F32)
-        ay[at_y(CY - 1, q), :] = jnp.zeros((CX, 128), F32)
-        my[at_y(CY - 1, q), :] = jnp.ones((CX, 128), F32)
+    for u in range(UNITS):
+        ht[at_y(CY - 1, u), :] = jnp.zeros((8, 128), F32)
+        ay[at_y(CY - 1, u), :] = jnp.zeros((8, 128), F32)
+        my[at_y(CY - 1, u), :] = jnp.ones((8, 128), F32)
     lax.fori_loop(0, CY // 8, finish, east_y)
 
     def drain_x(t):
         to = peer_x(t)
-        copy_x(xs.at[to], xr.at[me_x], xsem, to, to, me_x).wait_send()
-        copy_x(vs.at[to], vr.at[me_x], vsem, to, to, me_x).wait_send()
+        for q in range(4):
+            copy_x(xs.at[q, to], xr.at[q, me_x], xsem.at[q], to, to, me_x).wait_send()
+            copy_x(vs.at[q, to], vr.at[q, me_x], vsem.at[q], to, to, me_x).wait_send()
         copy_x(p1s.at[to], p1r.at[me_x], s1, to, to, me_x).wait_send()
         copy_x(gat.at[0], gb.at[me_x], sb, to, to, me_x).wait_send()
 
@@ -566,11 +571,26 @@
     each(GX, drain_x)
     each(GY, drain_y)
 
-    def drain_out(c):
-        for copy in out_copies(c):
-            copy.wait()
-
-    each(CY // 8, drain_out, 0)
+
+def deliver(staged, cur_in, out, cur_out, sems):
+    def copy(d, q):
+        return pltpu.make_async_copy(
+            staged.at[q, d], out.at[:, pl.ds(pl.multiple_of(d * 8, 8), 8), 128 * q : 128 * q + 128], sems.at[q, d]
+        )
+
+    def start(d, carry):
+        for q in range(4):
+            copy(d, q).start()
+        return carry
+
+    def wait(d, carry):
+        for q in range(4):
+            copy(d, q).wait()
+        return carry
+
+    lax.fori_loop(0, GX, start, 0)
+    cur_out[...] = cur_in[...]
+    lax.fori_loop(0, GX, wait, 0)
 
 
 def local(field, conduct, seg_cell, seg_count, currents, coupling):
@@ -581,15 +601,14 @@
     block = lambda *shape: pltpu.VMEM(shape, F32)
     sems = lambda count: pltpu.SemaphoreType.DMA((2, count))
     scratch = [
-        block(4, CX, CY, 128),
-        block(4, CX, CY, 128),
-        block(CX - 1, CY, NZ),
-        block(CX - 1, CY, NZ),
-        block(GX, 5, 8, NZ),
-        block(GX, 5, 8, NZ),
-        block(GX, 2, 8, NZ),
-        block(GX, 2, 8, NZ),
-        block(GX, 2, 8, NZ),
+        block(4, GX, CX, 8, 128),
+        block(4, GX, CX, 8, 128),
+        block(4, GX, CX, 8, 128),
+        block(4, GX, CX, 8, 128),
+        block(4, GX, 5, 8, 128),
+        block(4, GX, 5, 8, 128),
+        block(4, GX, 2, 8, 128),
+        block(4, GX, 2, 8, 128),
         block(4 * PLANE, 128),
         block(4 * PLANE, 128),
         block(4 * PLANE, 128),
@@ -599,6 +618,7 @@
         pltpu.VMEM((WIRE, NZ), BF16),
         block(WIRE, 128),
         pltpu.VMEM((128, 128), jnp.int32),
+        pltpu.SMEM((WIRE,), jnp.int32),
         block(GX, 8, 128),
         block(GX, 8, 128),
         block(GY, 8, 128),
@@ -616,8 +636,8 @@
         pltpu.SemaphoreType.DMA((GX, 4)),
         pltpu.SemaphoreType.DMA((GX, 4)),
         pltpu.SemaphoreType.DMA,
-        sems(GX),
-        sems(GX),
+        pltpu.SemaphoreType.DMA((4, 2, GX)),
+        pltpu.SemaphoreType.DMA((4, 2, GX)),
         sems(GX),
         sems(GY),
         sems(GY),
@@ -625,21 +645,31 @@
         sems(GY),
         sems(GY),
         sems(GY),
-        pltpu.SemaphoreType.DMA((CY // 8, 4)),
     ]
+    staged, currents_next = pl.pallas_call(
+        kernel,
+        out_shape=(
+            pltpu.VMEM((4, GX, CX, 8, 128), F32),
+            pltpu.VMEM((CAP, 128), F32),
+        ),
+        in_specs=[hbm, hbm, smem, vmem, vmem, vmem, hbm],
+        out_specs=(vmem, vmem),
+        scratch_shapes=scratch,
+        compiler_params=pltpu.CompilerParams(
+            collective_id=0, has_side_effects=True, vmem_limit_bytes=57 * 1024 * 1024
+        ),
+    )(field, conduct, cells, cells, seg_count, currents[0].T, coupling[0])
     field_next, currents_next = pl.pallas_call(
-        kernel,
+        deliver,
         out_shape=(
             jax.ShapeDtypeStruct((CX, CY, NZ), F32),
             jax.ShapeDtypeStruct((CAP, 128), F32),
         ),
-        in_specs=[hbm, hbm, smem, vmem, vmem, vmem, hbm],
+        in_specs=[pl.BlockSpec(memory_space=pl.ANY), vmem],
         out_specs=(hbm, vmem),
-        scratch_shapes=scratch,
-        compiler_params=pltpu.CompilerParams(
-            collective_id=0, has_side_effects=True, vmem_limit_bytes=56 * 1024 * 1024
-        ),
-    )(field, conduct, cells, cells, seg_count, currents[0].T, coupling[0])
+        scratch_shapes=[pltpu.SemaphoreType.DMA((4, GX))],
+        compiler_params=pltpu.CompilerParams(vmem_limit_bytes=4 * 1024 * 1024),
+    )(staged, currents_next)
     return field_next, currents_next.T[None]
 
 

time: 86.6 us -> 75 us (0.87)
  Pallas kernels: 80.4 us -> 74.2 us
  local copies, waits for them, and re-layouts: 5.39 us -> 0 us
    pallas_call x1 -> x2, Pallas kernels: 80.4 us -> 74.2 us  [the longest x1 71.1 us: local(): pl.pallas_call(kernel, out_shape=(pltpu.VMEM((4, GX, CX, 8, 128), F32), p...]
    unnamed x4 -> x0, local copies, waits for them, and re-layouts: 5.39 us -> none
where the time goes in v1:
time: 75 us; the launch traced here: 74.8 us
  Pallas kernels  74.2 us (99%)
    pallas_call x1, Pallas kernels, local(): pl.pallas_call(kernel, out_shape=(pltpu.VMEM((4, GX, CX, 8, 128), F32), p...  71.1 us
    pallas_call x1, Pallas kernels, local(): pl.pallas_call(deliver, out_shape=(jax.ShapeDtypeStruct((CX, CY, NZ), F32...  3.11 us

profile of v1, /device:TPU:1, one launch (start us, length us, event | category | flops | bytes accessed | tf_op | source)
XLA Modules:
  0.0 74.8 jit_solution(16394377713323708536)
XLA Ops:
  0.6 71.1 %shard_map.77 = (f32[4,16,16,8,128]{4,3,2,1,0:T(8,128)S(1)}, f32[4,128]{1,0:T(4,128)S(1)}) custom-call(f32[16,128,512]{2,1,0:T(8,128)} %field.1, f32[16,128,512]{2,1,0:T(8,128)} %conduct.1, s32[4,128]{1,0:T(4,128)} %bitcast.11, s32[4,128]{1,0:T(4,128)} %bitcast.12, s32[1,128]{1,0:T(1,128)} %count_v.1, f32[4,128]{1,0:T(4,128)} %bitcast.13, ...), custom_call_target="tpu_custom_call" | custom-call | tf_op jit(solution)/shard_map/pallas_call | solution.py:649
  71.7 3.1 %shard_map.78 = (f32[16,128,512]{2,1,0:T(8,128)}, f32[4,128]{1,0:T(4,128)}) custom-call(f32[4,16,16,8,128]{4,3,2,1,0:T(8,128)S(1)} %get-tuple-element.6.staged, f32[4,128]{1,0:T(4,128)S(1)} %get-tuple-element.7.cur_in), custom_call_target="tpu_custom_call" | custom-call | tf_op jit(solution)/shard_map/pallas_call | solution.py:662

commit v2 on v1

--- a/solution.py
+++ b/solution.py
@@ -19,7 +19,7 @@
 INJECT = 4.0 * KY**0.5
 PLANE = CY * CX
 UNITS = 8
-EARLY = 8
+EARLY = 2
 
 
 def inverse(value):
@@ -36,10 +36,9 @@
 def kernel(
     field,
     conduct,
-    cell_s,
-    cell_v,
-    count_v,
-    cur_v,
+    cell_h,
+    count_h,
+    cur_h,
     coupling,
     ob,
     cur_out,
@@ -56,11 +55,25 @@
     ay,
     cw,
     hot,
-    bh,
-    bl,
+    bhl,
     samp,
     zcol,
+    cell_v,
+    count_v,
+    cur_v,
+    rows_v,
     rows_s,
+    wv,
+    wp,
+    samp2,
+    pks,
+    pkr,
+    zhot,
+    xmask,
+    gbt,
+    yk,
+    added0,
+    added1,
     p1s,
     p1r,
     p2s,
@@ -87,6 +100,9 @@
     syc,
     syr,
     syv,
+    spk,
+    small,
+    rsem,
 ):
     me_x = lax.axis_index("gx")
     me_y = lax.axis_index("gy")
@@ -131,22 +147,28 @@
             copy.start()
         return carry
 
+    barrier = pltpu.get_barrier_semaphore()
+
+    def greet_x(t, carry):
+        pl.semaphore_signal(barrier, inc=1, device_id=(peer_x(t), me_y), device_id_type=MESH)
+        return carry
+
+    def greet_y(t, carry):
+        pl.semaphore_signal(barrier, inc=1, device_id=(me_x, peer_y(t)), device_id_type=MESH)
+        return carry
+
+    lax.fori_loop(1, GX, greet_x, 0)
+    lax.fori_loop(1, GY, greet_y, 0)
     lax.fori_loop(0, GX, start_in, 0)
     weights = pltpu.make_async_copy(coupling, cw, wsem)
     weights.start()
-
-    barrier = pltpu.get_barrier_semaphore()
-
-    def greet_x(t, carry):
-        pl.semaphore_signal(barrier, inc=1, device_id=(peer_x(t), me_y), device_id_type=MESH)
-        return carry
-
-    def greet_y(t, carry):
-        pl.semaphore_signal(barrier, inc=1, device_id=(me_x, peer_y(t)), device_id_type=MESH)
-        return carry
-
-    lax.fori_loop(1, GX, greet_x, 0)
-    lax.fori_loop(1, GY, greet_y, 0)
+    smalls = [
+        pltpu.make_async_copy(src, dst, small.at[i])
+        for i, (src, dst) in enumerate(((cell_h, cell_v), (count_h, count_v), (cur_h, cur_v)))
+    ]
+    for copy in smalls:
+        copy.start()
+
     def copy_x(src, dst, sems, slot, to, who):
         return pltpu.make_async_remote_copy(
             src_ref=src, dst_ref=dst, send_sem=sems.at[0, slot], recv_sem=sems.at[1, who],
@@ -249,6 +271,12 @@
         for slot, value in enumerate((a_y, g_y, gp_y)):
             ycs[u, slot] = value[u]
 
+    for u in range(UNITS):
+        my[at_y(CY - 1, u), :] = jnp.ones((8, 128), F32)
+        ay[at_y(CY - 1, u), :] = jnp.zeros((8, 128), F32)
+        wv[at_y(CY - 1, u), :] = jnp.ones((8, 128), F32)
+        wp[at_y(CY - 1, u), :] = jnp.zeros((8, 128), F32)
+
     def send_yc(t):
         to = peer_y(t)
         copy_y(ycs.at[to], ycr.at[me_y], syc, to, to, me_y).start()
@@ -256,20 +284,66 @@
     each(GY, send_yc)
     ycr[me_y] = ycs[me_y]
 
+    def weigh(n, state):
+        y = CY - 2 - n
+        to_last, to_west = state
+        last_new, west_new = [], []
+        for u in range(UNITS):
+            m = my[at_y(y, u), :]
+            last_new.append(m * to_last[u])
+            west_new.append(ay[at_y(y, u), :] + m * to_west[u])
+            wv[at_y(y, u), :] = last_new[u]
+            wp[at_y(y, u), :] = west_new[u]
+        return last_new, west_new
+
+    lax.fori_loop(0, CY - 1, weigh, (ones, zeros))
+
+    for copy in smalls:
+        copy.wait()
     cells = cell_v[...]
     slot_of = lax.broadcasted_iota(jnp.int32, (CAP, 128), 0)
     filled = slot_of < count_v[...]
+    at_x = cells >> 16
     place_z = jnp.where(filled, cells & (NZ - 1), -1)
-    place_r = (cells >> 19) * (8 * CY) + ((cells >> 9) & (CY - 1)) * 8 + ((cells >> 16) & 7)
+    place_r = ((cells >> 9) & (CY - 1)) * CX + at_x
+    rows_v[...] = ((cells >> 7) & 3) * PLANE + (at_x >> 3) * (8 * CY) + ((cells >> 9) & (CY - 1)) * 8 + (at_x & 7)
+    rows_copy = pltpu.make_async_copy(rows_v, rows_s, rsem)
+    rows_copy.start()
     zcol[...] = jnp.concatenate([place_z, jnp.full((128 - CAP, 128), -1, jnp.int32)], axis=0).T
-
-    def find(o):
-        for k in range(CAP):
-            c = cell_s[k, o]
-            row = ((c >> 7) & 3) * PLANE + (c >> 19) * (8 * CY) + ((c >> 9) & (CY - 1)) * 8 + ((c >> 16) & 7)
-            rows_s[k * 128 + o] = row
-
-    each(128, find, 0)
+    lanes = lax.broadcasted_iota(jnp.int32, (128, 128), 1)
+
+    def hit_of(k):
+        z = zcol[:, k : k + 1]
+        return ((z & 127) == lanes) & (z >= 0)
+
+    def pick(pairs):
+        def run(n):
+            for i in range(16):
+                o = n * 16 + i
+                for k in range(CAP):
+                    row = rows_s[k, o]
+                    for src, dst in pairs:
+                        dst[pl.ds(k * 128 + o, 1), :] = src[pl.ds(row, 1), :]
+
+        each(128 // 16, run, 0)
+
+    rows_copy.wait()
+    pick(((wv, samp), (wp, samp2)))
+    for k in range(CAP):
+        hit = hit_of(k)
+        rows = slice(128 * k, 128 * k + 128)
+        for slot, ref in enumerate((samp, samp2)):
+            chosen = jnp.where(hit, ref[rows, :], 0.0) * (INJECT / KY)
+            pks[slot * CAP + k : slot * CAP + k + 1, :] = jnp.sum(chosen.T, axis=0, keepdims=True)
+    pks[2 * CAP : 3 * CAP, :] = at_x.astype(F32)
+    pks[3 * CAP : 4 * CAP, :] = place_z.astype(F32)
+
+    def send_pk(t):
+        to = peer_y(t)
+        copy_y(pks, pkr.at[me_y], spk, to, to, me_y).start()
+
+    each(GY, send_pk)
+    pkr[me_y] = pks[...]
 
     def build_hot(n, carry):
         base = n * 128
@@ -361,19 +435,12 @@
     for q in range(4):
         substitute(q)
 
-    def take(n):
-        for i in range(16):
-            samp[pl.ds(n * 16 + i, 1), :] = ht[pl.ds(rows_s[n * 16 + i], 1), :]
-
-    each(WIRE // 16, take, 0)
-
-    lanes = lax.broadcasted_iota(jnp.int32, (128, 128), 1)
+    pick(((ht, samp),))
+
     mine = lax.rem(me_x, 4) * 32 + me_y * CAP
     placed = jnp.zeros((128, 128), F32)
     for k in range(CAP):
-        z = zcol[:, k : k + 1]
-        hit = ((z & 127) == lanes) & (z >= 0)
-        value = jnp.sum(jnp.where(hit, samp[128 * k : 128 * k + 128, :], 0.0), axis=1, keepdims=True) * KY
+        value = jnp.sum(jnp.where(hit_of(k), samp[128 * k : 128 * k + 128, :], 0.0), axis=1, keepdims=True) * KY
         placed = jnp.where(lanes == mine + k, value, placed)
     p1s[...] = placed.reshape(GX, GY, 128)
 
@@ -387,6 +454,26 @@
 
     each(GX, send_1)
     p1r[me_x] = p1s[me_x]
+    def sum_up(y, state):
+        f, fp = state
+        f_new, fp_new = [], []
+        for u in range(UNITS):
+            fp_new.append(fp[u] + ay[at_y(y, u), :] * f[u])
+            f_new.append(ht[at_y(y + 1, u), :] + f[u] * my[at_y(y, u), :])
+        return f_new, fp_new
+
+    first = [ht[at_y(0, u), :] for u in range(UNITS)]
+    f_y, fp_y = lax.fori_loop(0, CY - 1, sum_up, (first, zeros))
+    for u in range(UNITS):
+        for slot, value in enumerate((f_y, fp_y)):
+            yrs[u, slot] = value[u]
+
+    def send_yr(t):
+        to = peer_y(t)
+        copy_y(yrs.at[to], yrr.at[me_y], syr, to, to, me_y).start()
+
+    each(GY, send_yr)
+    yrr[me_y] = yrs[me_y]
     each(GX, arrive_1)
     for a in range(4):
         total = (p1r[4 * a] + p1r[4 * a + 1]) + (p1r[4 * a + 2] + p1r[4 * a + 3])
@@ -403,6 +490,38 @@
 
     each(GY, send_2)
     p2r[me_y] = p2s[me_y]
+    def arrive_pk(t):
+        frm = peer_y(t)
+        copy_y(pks, pkr.at[frm], spk, frm, frm, frm).wait_recv()
+
+    def arrive_yc(t):
+        frm = peer_y(t)
+        copy_y(ycs.at[frm], ycr.at[frm], syc, frm, frm, frm).wait_recv()
+
+    each(GY, arrive_pk)
+    each(GY, arrive_yc)
+    share_z = ((me_y // 2) * 128 + lax.broadcasted_iota(jnp.int32, (128, 128), 0)).astype(F32)
+    share_x = (lax.rem(me_y, 2) * 8 + lax.broadcasted_iota(jnp.int32, (8, 128), 0)).astype(F32)
+
+    def build_share(r):
+        info = pkr[r]
+        for k in range(CAP):
+            zhot[r, :, 128 * k : 128 * k + 128] = jnp.where(share_z == info[12 + k : 13 + k, :], 1.0, 0.0).astype(BF16)
+            match = share_x == info[8 + k : 9 + k, :]
+            for slot in range(2):
+                weight = info[4 * slot + k : 4 * slot + k + 1, :]
+                xmask[r, slot, :, 128 * k : 128 * k + 128] = jnp.where(match, weight, 0.0)
+
+    each(GY, build_share, 0)
+    q_y = ycr[0, 0] + ycr[0, 1] + ycr[1, 2]
+    for r in range(1, GY):
+        a = ycr[r, 0]
+        m = inverse(a + q_y)
+        yk[r, 0] = a * m
+        yk[r, 1] = m
+        more = ycr[r + 1, 2] if r < GY - 1 else 1.0
+        q_y = ycr[r, 1] + more + a * m * q_y
+    yk[0, 0] = inverse(q_y)
     each(GY, arrive_2)
     gathered = p2r[0]
     for j in range(1, GY):
@@ -441,93 +560,102 @@
 
     each(GX, send_b)
     gb[me_x] = gat[me_x // 4]
+    def drain_x(t):
+        to = peer_x(t)
+        for q in range(4):
+            copy_x(xs.at[q, to], xr.at[q, me_x], xsem.at[q], to, to, me_x).wait_send()
+            copy_x(vs.at[q, to], vr.at[q, me_x], vsem.at[q], to, to, me_x).wait_send()
+        copy_x(p1s.at[to], p1r.at[me_x], s1, to, to, me_x).wait_send()
+
+    def drain_y(t):
+        to = peer_y(t)
+        copy_y(p2s.at[to], p2r.at[me_y], s2, to, to, me_y).wait_send()
+        copy_y(ycs.at[to], ycr.at[me_y], syc, to, to, me_y).wait_send()
+        copy_y(yrs.at[to], yrr.at[me_y], syr, to, to, me_y).wait_send()
+        copy_y(pks, pkr.at[me_y], spk, to, to, me_y).wait_send()
+
+    each(GX, drain_x)
+    each(GY, drain_y)
     each(GX, arrive_b)
 
     back = gb[...].reshape(128, 128)
+    gbt[...] = back.T
+    mine_rows = gbt[pl.ds(pl.multiple_of(lax.rem(me_x, 4) * 32, 32), 32), :]
+    extra = []
+    for r in range(GY):
+        values = jnp.concatenate([mine_rows[CAP * r + k : CAP * r + k + 1, :] for k in range(CAP)], axis=1)
+        parts = jnp.concatenate([xmask[r, 0] * values, xmask[r, 1] * values], axis=0)
+        high = parts.astype(BF16)
+        low = (parts - high.astype(F32)).astype(BF16)
+        product = lax.dot_general(
+            jnp.concatenate([high, low], axis=0), zhot[r], (((1,), (1,)), ((), ())), preferred_element_type=F32
+        )
+        extra.append((product[0:8] + product[16:24], product[8:16] + product[24:32]))
+
+    def arrive_yr(t):
+        frm = peer_y(t)
+        copy_y(yrs.at[frm], yrr.at[frm], syr, frm, frm, frm).wait_recv()
+
+    each(GY, arrive_yr)
+    phi = (yrr[0, 0] + extra[0][0]) + (yrr[1, 1] + extra[1][1])
+    phis = [phi]
+    for r in range(1, GY):
+        phi = (yrr[r, 0] + extra[r][0]) + yk[r, 0] * phi
+        if r < GY - 1:
+            phi = phi + (yrr[r + 1, 1] + extra[r + 1][1])
+        phis.append(phi)
+    value = phi * yk[0, 0]
+    for r in range(GY - 1, 0, -1):
+        yvs[r, 1] = value
+        value = yk[r, 1] * phis[r - 1] + yk[r, 0] * value
+        yvs[r, 0] = value
+    yvs[0, 1] = value
+    yvs[0, 0] = jnp.zeros((8, 128), F32)
+
+    def send_yv(t):
+        to = peer_y(t)
+        copy_y(yvs.at[to], yvr.at[me_y], syv, to, to, me_y).start()
+
+    def arrive_yv(t):
+        frm = peer_y(t)
+        copy_y(yvs.at[frm], yvr.at[frm], syv, frm, frm, frm).wait_recv()
+
+    each(GY, send_yv)
+    yvr[me_y] = yvs[me_y]
+
     lane_k = lax.broadcasted_iota(jnp.int32, (128, NZ), 1)
     for k in range(CAP):
         value = jnp.sum(jnp.where(lanes == mine + k, back, 0.0), axis=1, keepdims=True) * (INJECT / KY)
         spot = jnp.where(lane_k == zcol[:, k : k + 1], value, 0.0)
         high = spot.astype(BF16)
-        bh[128 * k : 128 * k + 128, :] = high
-        bl[128 * k : 128 * k + 128, :] = (spot - high.astype(F32)).astype(BF16)
-
-    def scatter(n, carry):
-        rows = pl.ds(pl.multiple_of(n * 256, 256), 256)
-        part = hot[rows, :]
-        added = jnp.dot(part, bh[...], preferred_element_type=F32) + jnp.dot(part, bl[...], preferred_element_type=F32)
-        for q in range(4):
-            where = pl.ds(pl.multiple_of(q * PLANE + n * 256, 256), 256)
-            ht[where, :] = ht[where, :] + added[:, 128 * q : 128 * q + 128]
-        return carry
-
-    lax.fori_loop(0, PLANE // 256, scatter, 0)
-
-    def forward_y(y, state):
-        f, fp = state
-        f_new, fp_new = [], []
-        for u in range(UNITS):
-            b = f[u] * my[at_y(y, u), :]
-            fp_new.append(fp[u] + ay[at_y(y, u), :] * f[u])
-            f_new.append(ht[at_y(y + 1, u), :] + b)
-            ht[at_y(y, u), :] = b
-        return f_new, fp_new
-
-    first = [ht[at_y(0, u), :] for u in range(UNITS)]
-    f_y, fp_y = lax.fori_loop(0, CY - 1, forward_y, (first, zeros))
-    for u in range(UNITS):
-        for slot, value in enumerate((f_y, fp_y)):
-            yrs[u, slot] = value[u]
-
-    def send_yr(t):
-        to = peer_y(t)
-        copy_y(yrs.at[to], yrr.at[me_y], syr, to, to, me_y).start()
-
-    def arrive_yr(t):
-        frm = peer_y(t)
-        copy_y(yrs.at[frm], yrr.at[frm], syr, frm, frm, frm).wait_recv()
-
-    def arrive_yc(t):
-        frm = peer_y(t)
-        copy_y(ycs.at[frm], ycr.at[frm], syc, frm, frm, frm).wait_recv()
-
-    each(GY, send_yr)
-    yrr[me_y] = yrs[me_y]
-    each(GY, arrive_yc)
-    m_list = [None]
-    q_y = ycr[0, 0] + ycr[0, 1] + ycr[1, 2]
-    for r in range(1, GY):
-        a = ycr[r, 0]
-        m = inverse(a + q_y)
-        m_list.append((a * m, m))
-        more = ycr[r + 1, 2] if r < GY - 1 else 1.0
-        q_y = ycr[r, 1] + more + a * m * q_y
-    last = inverse(q_y)
-    each(GY, arrive_yr)
-    phi = yrr[0, 0] + yrr[1, 1]
-    phis = [phi]
-    for r in range(1, GY):
-        more = yrr[r + 1, 1] if r < GY - 1 else 0.0
-        phi = yrr[r, 0] + more + m_list[r][0] * phi
-        phis.append(phi)
-    value = phi * last
-    for r in range(GY - 1, 0, -1):
-        yvs[r, 1] = value
-        value = m_list[r][1] * phis[r - 1] + m_list[r][0] * value
-        yvs[r, 0] = value
-    yvs[0, 1] = value
-    yvs[0, 0] = jnp.zeros((8, 128), F32)
-
-    def send_yv(t):
-        to = peer_y(t)
-        copy_y(yvs.at[to], yvr.at[me_y], syv, to, to, me_y).start()
-
-    def arrive_yv(t):
-        frm = peer_y(t)
-        copy_y(yvs.at[frm], yvr.at[frm], syv, frm, frm, frm).wait_recv()
-
-    each(GY, send_yv)
-    yvr[me_y] = yvs[me_y]
+        bhl[128 * k : 128 * k + 128, :] = high
+        bhl[WIRE + 128 * k : WIRE + 128 * k + 128, :] = (spot - high.astype(F32)).astype(BF16)
+
+    def scatter(n, added):
+        part = hot[pl.ds(pl.multiple_of(n * 256, 256), 256), :]
+        added[...] = jnp.dot(jnp.concatenate([part, part], axis=1), bhl[...], preferred_element_type=F32)
+
+    def eliminate_y(n, added, state):
+        for step in range(16):
+            y = n * 16 + step
+            new = []
+            for u in range(UNITS):
+                row = step * CX + (u % 2) * 8
+                more = added[row : row + 8, quarter(u // 2)]
+                b = ((ht[at_y(y, u), :] + more) + state[u]) * my[at_y(y, u), :]
+                ht[at_y(y, u), :] = b
+                new.append(b)
+            state = new
+        return state
+
+    def forward_y(n, state):
+        scatter(2 * n + 1, added1)
+        state = eliminate_y(2 * n, added0, state)
+        scatter(jnp.minimum(2 * n + 2, CY // 16 - 1), added0)
+        return eliminate_y(2 * n + 1, added1, state)
+
+    scatter(0, added0)
+    lax.fori_loop(0, CY // 32, forward_y, zeros)
     each(GY, arrive_yv)
 
     west_y = [yvr[u, 0] for u in range(UNITS)]
@@ -548,28 +676,18 @@
 
     for u in range(UNITS):
         ht[at_y(CY - 1, u), :] = jnp.zeros((8, 128), F32)
-        ay[at_y(CY - 1, u), :] = jnp.zeros((8, 128), F32)
-        my[at_y(CY - 1, u), :] = jnp.ones((8, 128), F32)
     lax.fori_loop(0, CY // 8, finish, east_y)
 
-    def drain_x(t):
-        to = peer_x(t)
-        for q in range(4):
-            copy_x(xs.at[q, to], xr.at[q, me_x], xsem.at[q], to, to, me_x).wait_send()
-            copy_x(vs.at[q, to], vr.at[q, me_x], vsem.at[q], to, to, me_x).wait_send()
-        copy_x(p1s.at[to], p1r.at[me_x], s1, to, to, me_x).wait_send()
-        copy_x(gat.at[0], gb.at[me_x], sb, to, to, me_x).wait_send()
-
-    def drain_y(t):
+    def drain_late_x(t):
+        copy_x(gat.at[0], gb.at[me_x], sb, peer_x(t), peer_x(t), me_x).wait_send()
+
+    def drain_late_y(t):
         to = peer_y(t)
-        copy_y(p2s.at[to], p2r.at[me_y], s2, to, to, me_y).wait_send()
         copy_y(ys, ga.at[me_y], sa, to, to, me_y).wait_send()
-        copy_y(ycs.at[to], ycr.at[me_y], syc, to, to, me_y).wait_send()
-        copy_y(yrs.at[to], yrr.at[me_y], syr, to, to, me_y).wait_send()
         copy_y(yvs.at[to], yvr.at[me_y], syv, to, to, me_y).wait_send()
 
-    each(GX, drain_x)
-    each(GY, drain_y)
+    each(GX, drain_late_x)
+    each(GY, drain_late_y)
 
 
 def deliver(staged, cur_in, out, cur_out, sems):
@@ -596,7 +714,6 @@
 def local(field, conduct, seg_cell, seg_count, currents, coupling):
     hbm = pl.BlockSpec(memory_space=pltpu.HBM)
     vmem = pl.BlockSpec(memory_space=pltpu.VMEM)
-    smem = pl.BlockSpec(memory_space=pltpu.SMEM)
     cells = seg_cell[0].T
     block = lambda *shape: pltpu.VMEM(shape, F32)
     sems = lambda count: pltpu.SemaphoreType.DMA((2, count))
@@ -614,11 +731,25 @@
         block(4 * PLANE, 128),
         pltpu.VMEM((WIRE, WIRE), BF16),
         pltpu.VMEM((PLANE, WIRE), BF16),
-        pltpu.VMEM((WIRE, NZ), BF16),
-        pltpu.VMEM((WIRE, NZ), BF16),
+        pltpu.VMEM((2 * WIRE, NZ), BF16),
         block(WIRE, 128),
         pltpu.VMEM((128, 128), jnp.int32),
-        pltpu.SMEM((WIRE,), jnp.int32),
+        pltpu.VMEM((CAP, 128), jnp.int32),
+        pltpu.VMEM((1, 128), jnp.int32),
+        block(CAP, 128),
+        pltpu.VMEM((CAP, 128), jnp.int32),
+        pltpu.SMEM((CAP, 128), jnp.int32),
+        block(4 * PLANE, 128),
+        block(4 * PLANE, 128),
+        block(WIRE, 128),
+        block(16, 128),
+        block(GY, 16, 128),
+        pltpu.VMEM((GY, 128, WIRE), BF16),
+        block(GY, 2, 8, WIRE),
+        block(128, 128),
+        block(GY, 2, 8, 128),
+        block(256, NZ),
+        block(256, NZ),
         block(GX, 8, 128),
         block(GX, 8, 128),
         block(GY, 8, 128),
@@ -645,6 +776,9 @@
         sems(GY),
         sems(GY),
         sems(GY),
+        sems(GY),
+        pltpu.SemaphoreType.DMA((3,)),
+        pltpu.SemaphoreType.DMA,
     ]
     staged, currents_next = pl.pallas_call(
         kernel,
@@ -652,13 +786,13 @@
             pltpu.VMEM((4, GX, CX, 8, 128), F32),
             pltpu.VMEM((CAP, 128), F32),
         ),
-        in_specs=[hbm, hbm, smem, vmem, vmem, vmem, hbm],
+        in_specs=[hbm] * 6,
         out_specs=(vmem, vmem),
         scratch_shapes=scratch,
         compiler_params=pltpu.CompilerParams(
             collective_id=0, has_side_effects=True, vmem_limit_bytes=57 * 1024 * 1024
         ),
-    )(field, conduct, cells, cells, seg_count, currents[0].T, coupling[0])
+    )(field, conduct, cells, seg_count, currents[0].T, coupling[0])
     field_next, currents_next = pl.pallas_call(
         deliver,
         out_shape=(

time: 75 us -> 66.3 us (0.88)
  Pallas kernels: 74.2 us -> 65.5 us
    pallas_call x1, Pallas kernels: 71.1 us -> 62.4 us  [local(): pl.pallas_call(kernel, out_shape=(pltpu.VMEM((4, GX, CX, 8, 128), F32), p...]
where the time goes in v2:
time: 66.3 us; the launch traced here: 66.2 us
  Pallas kernels  65.5 us (99%)
    pallas_call x1, Pallas kernels, local(): pl.pallas_call(kernel, out_shape=(pltpu.VMEM((4, GX, CX, 8, 128), F32), p...  62.4 us
    pallas_call x1, Pallas kernels, local(): pl.pallas_call(deliver, out_shape=(jax.ShapeDtypeStruct((CX, CY, NZ), F32...  3.11 us

profile of v2, /device:TPU:1, one launch (start us, length us, event | category | flops | bytes accessed | tf_op | source)
XLA Modules:
  0.0 66.2 jit_solution(1944440201246082715)
XLA Ops:
  0.6 62.4 %shard_map.77 = (f32[4,16,16,8,128]{4,3,2,1,0:T(8,128)S(1)}, f32[4,128]{1,0:T(4,128)S(1)}) custom-call(f32[16,128,512]{2,1,0:T(8,128)} %field.1, f32[16,128,512]{2,1,0:T(8,128)} %conduct.1, s32[4,128]{1,0:T(4,128)} %bitcast.11, s32[1,128]{1,0:T(1,128)} %count_h.1, f32[4,128]{1,0:T(4,128)} %bitcast.12, bf16[512,512]{1,0:T(8,128)(2,1)} %bitcast.10), custom_call_target="tpu_custom_call" | custom-call | tf_op jit(solution)/shard_map/pallas_call | solution.py:783
  63.1 3.1 %shard_map.78 = (f32[16,128,512]{2,1,0:T(8,128)}, f32[4,128]{1,0:T(4,128)}) custom-call(f32[4,16,16,8,128]{4,3,2,1,0:T(8,128)S(1)} %get-tuple-element.6.staged, f32[4,128]{1,0:T(4,128)S(1)} %get-tuple-element.7.cur_in), custom_call_target="tpu_custom_call" | custom-call | tf_op jit(solution)/shard_map/pallas_call | solution.py:796

commit v3 on v2

--- a/solution.py
+++ b/solution.py
@@ -63,6 +63,15 @@
     cur_v,
     rows_v,
     rows_s,
+    rows_n,
+    rows_t,
+    samp3,
+    pas,
+    par,
+    lines,
+    acc,
+    tmat,
+    cw2,
     wv,
     wp,
     samp2,
@@ -101,6 +110,7 @@
     syr,
     syv,
     spk,
+    spa,
     small,
     rsem,
 ):
@@ -184,61 +194,131 @@
     lane_z = lax.broadcasted_iota(jnp.int32, (8, NZ), 1)
     scale_f = 1.0 / (KX * KY)
 
-    def eliminate(d):
-        for copy in in_copies(d):
-            copy.wait()
-
-        def ground(x):
+    def eliminate(ds):
+        for d in ds:
+            for copy in in_copies(d):
+                copy.wait()
+
+        def ground(d, x):
             return (1.0 / KX) + (0.5 / KX) * load4(cb, d, x)
 
-        def source(x):
+        def source(d, x):
             value = load4(fb, d, x)
             up = jnp.where(lane_z == NZ - 1, 0.0, pltpu.roll(value, NZ - 1, 1))
             down = jnp.where(lane_z == 0, 0.0, pltpu.roll(value, 1, 1))
             return (0.5 * scale_f) * value + (0.25 * scale_f) * (up + down)
 
-        a = jnp.ones((8, NZ), F32)
-        g = ground(0)
-        f = source(0)
-        gp = jnp.zeros((8, NZ), F32)
-        fp = jnp.zeros((8, NZ), F32)
+        blank4 = jnp.zeros((8, NZ), F32)
+        states = [(jnp.ones((8, NZ), F32), ground(d, 0), source(d, 0), blank4, blank4) for d in ds]
         for x in range(CX - 1):
-            m = inverse(a + g + 1.0)
-            am = a * m
-            b = f * m
-            gp = gp + am * g
-            fp = fp + am * f
-            f = source(x + 1) + b
-            for q in range(4):
-                mx[q, d, x] = m[:, quarter(q)]
-                ax[q, d, x] = am[:, quarter(q)]
-                fb[q, d, x] = b[:, quarter(q)]
-            g = ground(x + 1) + g * m
-            a = am
-        for slot, value in enumerate((a, g, f, gp, fp)):
-            for q in range(4):
-                xs[q, d, slot] = value[:, quarter(q)]
+            for n, d in enumerate(ds):
+                a, g, f, gp, fp = states[n]
+                m = inverse(a + g + 1.0)
+                am = a * m
+                b = f * m
+                gp = gp + am * g
+                fp = fp + am * f
+                f = source(d, x + 1) + b
+                for q in range(4):
+                    mx[q, d, x] = m[:, quarter(q)]
+                    ax[q, d, x] = am[:, quarter(q)]
+                    fb[q, d, x] = b[:, quarter(q)]
+                states[n] = (am, ground(d, x + 1) + g * m, f, gp, fp)
+        for n, d in enumerate(ds):
+            for slot, value in enumerate(states[n]):
+                for q in range(4):
+                    xs[q, d, slot] = value[:, quarter(q)]
 
     def send_x(q, d):
         copy_x(xs.at[q, d], xr.at[q, me_x], xsem.at[q], d, d, me_x).start()
 
     def eliminate_and_send(t):
         d = order(t)
-        eliminate(d)
+        eliminate([d])
 
         @pl.when(t < GX - 1)
         def _():
             send_x(0, d)
 
-    each(EARLY, lambda t: eliminate(order(t)), 0)
+    each(EARLY, lambda t: eliminate([order(t)]), 0)
     pl.semaphore_wait(barrier, GX - 1 + GY - 1)
     each(EARLY, lambda t: send_x(0, order(t)), 0)
     each(GX, eliminate_and_send, EARLY)
-    for q in range(1, 4):
+    for q in range(1, 3):
         each(GX - 1, lambda t, q=q: send_x(q, order(t)), 0)
     for q in range(4):
         xr[q, me_x] = xs[q, me_x]
 
+    def respond(d):
+        own = jnp.zeros((8, NZ), F32)
+        west = jnp.zeros((8, NZ), F32)
+        last = jnp.ones((8, NZ), F32)
+        for x in range(CX - 1, -1, -1):
+            if x < CX - 1:
+                m = load4(mx, d, x)
+                own = load4(fb, d, x) + m * own
+                west = load4(ax, d, x) + m * west
+                last = m * last
+            for q in range(4):
+                fb[q, d, x] = own[:, quarter(q)]
+                ax[q, d, x] = west[:, quarter(q)]
+                mx[q, d, x] = last[:, quarter(q)]
+
+    each(GX, respond, 0)
+
+    for copy in smalls:
+        copy.wait()
+    cells = cell_v[...]
+    slot_of = lax.broadcasted_iota(jnp.int32, (CAP, 128), 0)
+    filled = slot_of < count_v[...]
+    at_x = cells >> 16
+    place_z = jnp.where(filled, cells & (NZ - 1), -1)
+    place_r = ((cells >> 9) & (CY - 1)) * CX + at_x
+    rows_v[...] = ((cells >> 7) & 3) * PLANE + (at_x >> 3) * (8 * CY) + ((cells >> 9) & (CY - 1)) * 8 + (at_x & 7)
+    rows_n[...] = ((cells >> 7) & 3) * PLANE + ((cells >> 12) & 15) * 128 + at_x * 8 + ((cells >> 9) & 7)
+    rows_copies = [
+        pltpu.make_async_copy(rows_n, rows_t, rsem.at[0]),
+        pltpu.make_async_copy(rows_v, rows_s, rsem.at[1]),
+    ]
+    for copy in rows_copies:
+        copy.start()
+    zcol[...] = jnp.concatenate([place_z, jnp.full((128 - CAP, 128), -1, jnp.int32)], axis=0).T
+    lanes = lax.broadcasted_iota(jnp.int32, (128, 128), 1)
+
+    def hit_of(k):
+        z = zcol[:, k : k + 1]
+        return ((z & 127) == lanes) & (z >= 0)
+
+    def pick(table, pairs):
+        def run(n):
+            for i in range(16):
+                o = n * 16 + i
+                for k in range(CAP):
+                    row = table[k, o]
+                    for src, dst in pairs:
+                        dst[pl.ds(k * 128 + o, 1), :] = src[pl.ds(row, 1), :]
+
+        each(128 // 16, run, 0)
+
+    rows_copies[0].wait()
+    pick(rows_t, [(ref.reshape(4 * PLANE, 128), dst) for ref, dst in ((fb, samp), (ax, samp2), (mx, samp3))])
+    for k in range(CAP):
+        hit = hit_of(k)
+        rows = slice(128 * k, 128 * k + 128)
+        for slot, ref in enumerate((samp, samp2, samp3)):
+            chosen = jnp.where(hit, ref[rows, :], 0.0) * KY
+            pas[slot * CAP + k : slot * CAP + k + 1, :] = jnp.sum(chosen.T, axis=0, keepdims=True)
+    key = ((cells >> 12) & 15) * 32 + ((cells >> 7) & 3) * 8 + ((cells >> 9) & 7)
+    pas[3 * CAP : 4 * CAP, :] = (key * 128 + (cells & 127)).astype(F32)
+
+    def send_pa(t):
+        to = order(t)
+        copy_x(pas, par.at[me_x], spa, to, to, me_x).start()
+
+    each(GX - 1, send_pa, 0)
+    par[me_x] = pas[...]
+    each(GX - 1, lambda t: send_x(3, order(t)), 0)
+
     cb2 = cb.reshape(4 * PLANE, 128)
 
     def spread_rows(y, u):
@@ -250,8 +330,17 @@
     def at_y(y, u):
         return pl.ds(pl.multiple_of(u * (8 * CY) + y * 8, 8), 8)
 
+    row_16 = lax.broadcasted_iota(jnp.int32, (CX, 128), 0)
+
+    def build_hot(y):
+        rows = row_16 + y * CX
+        for k in range(CAP):
+            match = jnp.where(rows == place_r[k : k + 1, :], 1.0, 0.0)
+            hot[pl.ds(pl.multiple_of(y * CX, CX), CX), quarter(k)] = match.astype(BF16)
+
     def factor(y, state):
         a, g, gp = state
+        build_hot(y)
         after = ground_y(y + 1)
         a_new, g_new, gp_new = [], [], []
         for u in range(UNITS):
@@ -267,6 +356,7 @@
     ones = [jnp.ones((8, 128), F32) for _ in range(UNITS)]
     zeros = [jnp.zeros((8, 128), F32) for _ in range(UNITS)]
     a_y, g_y, gp_y = lax.fori_loop(0, CY - 1, factor, (ones, ground_y(0), zeros))
+    build_hot(CY - 1)
     for u in range(UNITS):
         for slot, value in enumerate((a_y, g_y, gp_y)):
             ycs[u, slot] = value[u]
@@ -298,37 +388,8 @@
 
     lax.fori_loop(0, CY - 1, weigh, (ones, zeros))
 
-    for copy in smalls:
-        copy.wait()
-    cells = cell_v[...]
-    slot_of = lax.broadcasted_iota(jnp.int32, (CAP, 128), 0)
-    filled = slot_of < count_v[...]
-    at_x = cells >> 16
-    place_z = jnp.where(filled, cells & (NZ - 1), -1)
-    place_r = ((cells >> 9) & (CY - 1)) * CX + at_x
-    rows_v[...] = ((cells >> 7) & 3) * PLANE + (at_x >> 3) * (8 * CY) + ((cells >> 9) & (CY - 1)) * 8 + (at_x & 7)
-    rows_copy = pltpu.make_async_copy(rows_v, rows_s, rsem)
-    rows_copy.start()
-    zcol[...] = jnp.concatenate([place_z, jnp.full((128 - CAP, 128), -1, jnp.int32)], axis=0).T
-    lanes = lax.broadcasted_iota(jnp.int32, (128, 128), 1)
-
-    def hit_of(k):
-        z = zcol[:, k : k + 1]
-        return ((z & 127) == lanes) & (z >= 0)
-
-    def pick(pairs):
-        def run(n):
-            for i in range(16):
-                o = n * 16 + i
-                for k in range(CAP):
-                    row = rows_s[k, o]
-                    for src, dst in pairs:
-                        dst[pl.ds(k * 128 + o, 1), :] = src[pl.ds(row, 1), :]
-
-        each(128 // 16, run, 0)
-
-    rows_copy.wait()
-    pick(((wv, samp), (wp, samp2)))
+    rows_copies[1].wait()
+    pick(rows_s, [(wv, samp), (wp, samp2)])
     for k in range(CAP):
         hit = hit_of(k)
         rows = slice(128 * k, 128 * k + 128)
@@ -344,36 +405,6 @@
 
     each(GY, send_pk)
     pkr[me_y] = pks[...]
-
-    def build_hot(n, carry):
-        base = n * 128
-        rows = lax.broadcasted_iota(jnp.int32, (128, 128), 0) + base
-        for k in range(CAP):
-            match = jnp.where(rows == place_r[k : k + 1, :], 1.0, 0.0)
-            hot[pl.ds(pl.multiple_of(base, 128), 128), 128 * k : 128 * k + 128] = match.astype(BF16)
-        return carry
-
-    lax.fori_loop(0, PLANE // 128, build_hot, 0)
-
-    row_m = lax.broadcasted_iota(jnp.int32, (128, WIRE), 0)
-    lane_m = lax.broadcasted_iota(jnp.int32, (128, WIRE), 1)
-    spread = [jnp.where(lane_m == row_m * CAP + k, 1.0, 0.0).astype(BF16) for k in range(CAP)]
-
-    def three_rows(row):
-        high, middle, low = split3(row)
-        index = lax.broadcasted_iota(jnp.int32, (16, row.shape[1]), 0)
-        stack = jnp.where(index == 0, high, jnp.where(index == 1, middle, jnp.where(index == 2, low, 0.0)))
-        return stack.astype(BF16)
-
-    def exact_dot(row, matrix, dims):
-        product = lax.dot_general(three_rows(row), matrix, (dims, ((), ())), preferred_element_type=F32)
-        return (product[2:3] + product[1:2]) + product[0:1]
-
-    cur_row = jnp.zeros((1, WIRE), F32)
-    for k in range(CAP):
-        cur_row = cur_row + exact_dot(cur_v[k : k + 1, :], spread[k], ((1,), (0,)))
-    p2s[...] = jnp.zeros_like(p2s)
-    ys[...] = jnp.zeros_like(ys)
 
     blank = jnp.zeros((8, 128), F32)
 
@@ -402,6 +433,7 @@
         vs[q, 0, 1] = value
         vs[q, 0, 0] = blank
 
+    def send_back(q):
         def send(t):
             to = peer_x(t)
             copy_x(vs.at[q, to], vr.at[q, me_x], vsem.at[q], to, to, me_x).start()
@@ -409,8 +441,105 @@
         each(GX, send)
         vr[q, me_x] = vs[q, me_x]
 
-    for q in range(4):
-        reduce_x(q)
+    row_8 = lax.broadcasted_iota(jnp.int32, (8, 128), 0)
+    row_128 = lax.broadcasted_iota(jnp.int32, (128, 128), 0)
+
+    def build_lines(r):
+        code = par[r, 3 * CAP : 4 * CAP, :].astype(jnp.int32)
+        for k in range(CAP):
+            match = jnp.where(row_128 == (code[k : k + 1, :] & 127), 1.0, 0.0)
+            lines[r, :, quarter(k)] = match.astype(BF16)
+
+    def gather_x(quarters, first):
+        def one(r):
+            info = par[r]
+            code = info[3 * CAP : 4 * CAP, :].astype(jnp.int32)
+            parts = []
+            for q in quarters:
+                value = vs[q, r].reshape(16, 128)
+                high = value.astype(BF16).astype(F32)
+                parts.extend((high, value - high))
+            product = jnp.dot(jnp.concatenate(parts, axis=0).astype(BF16), lines[r], preferred_element_type=F32)
+            for k in range(CAP):
+                total = jnp.zeros((8, 128), F32) if first else acc[r, :, quarter(k)]
+                for n, q in enumerate(quarters):
+                    solved = product[32 * n : 32 * n + 16, quarter(k)] + product[32 * n + 16 : 32 * n + 32, quarter(k)]
+                    match = (code[k : k + 1, :] >> 7) == me_x * 32 + q * 8 + row_8
+                    value = (
+                        info[k : k + 1, :]
+                        + info[CAP + k : CAP + k + 1, :] * solved[0:8]
+                        + info[2 * CAP + k : 2 * CAP + k + 1, :] * solved[8:16]
+                    )
+                    total = total + jnp.where(match, value, 0.0)
+                acc[r, :, quarter(k)] = total
+
+        def four(n):
+            for i in range(4):
+                one(n * 4 + i)
+
+        each(4, four, 0)
+
+    reduce_x(0)
+    send_back(0)
+    reduce_x(1)
+    send_back(1)
+
+    def arrive_pa(t):
+        frm = peer_x(t)
+        copy_x(pas, par.at[frm], spa, frm, frm, frm).wait_recv()
+
+    each(GX, arrive_pa)
+    each(GX, build_lines, 0)
+    reduce_x(2)
+    send_back(2)
+    gather_x((0, 1, 2), True)
+    reduce_x(3)
+    gather_x((3,), False)
+
+    tmat[...] = jnp.zeros_like(tmat)
+    p2s[...] = jnp.zeros_like(p2s)
+    ys[...] = jnp.zeros_like(ys)
+    mine = lax.rem(me_x, 4) * 32 + me_y * CAP
+    for r in range(GX):
+        total = jnp.sum(acc[r], axis=0, keepdims=True)
+        for k in range(CAP):
+            tmat[pl.ds(lax.rem(me_y, 2) * 64 + CAP * r + k, 1), :] = total[:, quarter(k)]
+    p1s[...] = tmat[...].T.reshape(GX, GY, 128)
+
+    def send_1(t):
+        to = peer_x(t)
+        copy_x(p1s.at[to], p1r.at[me_x], s1, to, to, me_x).start()
+
+    def arrive_1(t):
+        frm = peer_x(t)
+        copy_x(p1s.at[frm], p1r.at[frm], s1, frm, frm, frm).wait_recv()
+
+    each(GX, send_1)
+    p1r[me_x] = p1s[me_x]
+    send_back(3)
+
+    row_m = lax.broadcasted_iota(jnp.int32, (128, WIRE), 0)
+    lane_m = lax.broadcasted_iota(jnp.int32, (128, WIRE), 1)
+    spread = [jnp.where(lane_m == row_m * CAP + k, 1.0, 0.0).astype(BF16) for k in range(CAP)]
+
+    def three_rows(row):
+        high, middle, low = split3(row)
+        index = lax.broadcasted_iota(jnp.int32, (16, row.shape[1]), 0)
+        stack = jnp.where(index == 0, high, jnp.where(index == 1, middle, jnp.where(index == 2, low, 0.0)))
+        return stack.astype(BF16)
+
+    def exact_dot(row, matrix, dims):
+        product = lax.dot_general(three_rows(row), matrix, (dims, ((), ())), preferred_element_type=F32)
+        return (product[2:3] + product[1:2]) + product[0:1]
+
+    cur_row = jnp.zeros((1, WIRE), F32)
+    for k in range(CAP):
+        cur_row = cur_row + exact_dot(cur_v[k : k + 1, :], spread[k], ((1,), (0,)))
+    lane_n = lax.broadcasted_iota(jnp.int32, (WIRE, WIRE), 1)
+    source_n = ((lane_n >> 2) & 15) * 32 + (lane_n >> 6) * CAP + (lane_n & 3)
+    shuffle = jnp.where(lax.broadcasted_iota(jnp.int32, (WIRE, WIRE), 0) == source_n, 1.0, 0.0).astype(BF16)
+    weights.wait()
+    cw2[...] = jnp.dot(cw[...], shuffle, preferred_element_type=F32).astype(BF16)
 
     def substitute(q):
         def arrive(t):
@@ -420,65 +549,25 @@
         def group(n):
             ds = [n * 4 + i for i in range(4)]
             west = [vr[q, d, 0] for d in ds]
-            value = [vr[q, d, 1] for d in ds]
-            for x in range(CX - 1, -1, -1):
-                if x < CX - 1:
-                    value = [
-                        (fb[q, d, x] + ax[q, d, x] * west[i]) + mx[q, d, x] * value[i] for i, d in enumerate(ds)
-                    ]
+            last = [vr[q, d, 1] for d in ds]
+            for x in range(CX):
+                value = [
+                    (fb[q, d, x] + ax[q, d, x] * west[i]) + mx[q, d, x] * last[i] for i, d in enumerate(ds)
+                ]
                 for i, d in enumerate(ds):
                     ht[pl.ds((2 * q + x // 8) * (8 * CY) + d * 64 + x % 8, 8, stride=8), :] = value[i]
 
         each(GX, arrive)
         each(4, group, 0)
 
-    for q in range(4):
-        substitute(q)
-
-    pick(((ht, samp),))
-
-    mine = lax.rem(me_x, 4) * 32 + me_y * CAP
-    placed = jnp.zeros((128, 128), F32)
-    for k in range(CAP):
-        value = jnp.sum(jnp.where(hit_of(k), samp[128 * k : 128 * k + 128, :], 0.0), axis=1, keepdims=True) * KY
-        placed = jnp.where(lanes == mine + k, value, placed)
-    p1s[...] = placed.reshape(GX, GY, 128)
-
-    def send_1(t):
-        to = peer_x(t)
-        copy_x(p1s.at[to], p1r.at[me_x], s1, to, to, me_x).start()
-
-    def arrive_1(t):
-        frm = peer_x(t)
-        copy_x(p1s.at[frm], p1r.at[frm], s1, frm, frm, frm).wait_recv()
-
-    each(GX, send_1)
-    p1r[me_x] = p1s[me_x]
-    def sum_up(y, state):
-        f, fp = state
-        f_new, fp_new = [], []
-        for u in range(UNITS):
-            fp_new.append(fp[u] + ay[at_y(y, u), :] * f[u])
-            f_new.append(ht[at_y(y + 1, u), :] + f[u] * my[at_y(y, u), :])
-        return f_new, fp_new
-
-    first = [ht[at_y(0, u), :] for u in range(UNITS)]
-    f_y, fp_y = lax.fori_loop(0, CY - 1, sum_up, (first, zeros))
-    for u in range(UNITS):
-        for slot, value in enumerate((f_y, fp_y)):
-            yrs[u, slot] = value[u]
-
-    def send_yr(t):
-        to = peer_y(t)
-        copy_y(yrs.at[to], yrr.at[me_y], syr, to, to, me_y).start()
-
-    each(GY, send_yr)
-    yrr[me_y] = yrs[me_y]
+    substitute(0)
+    substitute(1)
     each(GX, arrive_1)
-    for a in range(4):
-        total = (p1r[4 * a] + p1r[4 * a + 1]) + (p1r[4 * a + 2] + p1r[4 * a + 3])
-        for j in range(GY):
-            p2s[j, a : a + 1, :] = total[j : j + 1, :]
+    total = p1r[0]
+    for i in range(1, GX):
+        total = total + p1r[i]
+    for j in range(GY):
+        p2s[j, 0:1, :] = total[j : j + 1, :]
 
     def send_2(t):
         to = peer_y(t)
@@ -522,13 +611,10 @@
         more = ycr[r + 1, 2] if r < GY - 1 else 1.0
         q_y = ycr[r, 1] + more + a * m * q_y
     yk[0, 0] = inverse(q_y)
+    substitute(2)
     each(GY, arrive_2)
-    gathered = p2r[0]
-    for j in range(1, GY):
-        gathered = gathered + p2r[j]
-    row = jnp.concatenate([gathered[a : a + 1, :] for a in range(4)], axis=1)
-    weights.wait()
-    new_row = 0.5 * cur_row + exact_dot(row, cw[...], ((1,), (1,)))
+    row = jnp.concatenate([p2r[2 * j, 0:1, :] + p2r[2 * j + 1, 0:1, :] for j in range(4)], axis=1)
+    new_row = 0.5 * cur_row + exact_dot(row, cw2[...], ((1,), (1,)))
     for a in range(4):
         ys[a : a + 1, :] = new_row[:, 128 * a : 128 * a + 128]
 
@@ -544,6 +630,27 @@
     ga[me_y] = ys[...]
     for k in range(CAP):
         cur_out[k : k + 1, :] = exact_dot(new_row, spread[k], ((1,), (1,)))
+    substitute(3)
+    def sum_up(y, state):
+        f, fp = state
+        f_new, fp_new = [], []
+        for u in range(UNITS):
+            fp_new.append(fp[u] + ay[at_y(y, u), :] * f[u])
+            f_new.append(ht[at_y(y + 1, u), :] + f[u] * my[at_y(y, u), :])
+        return f_new, fp_new
+
+    first = [ht[at_y(0, u), :] for u in range(UNITS)]
+    f_y, fp_y = lax.fori_loop(0, CY - 1, sum_up, (first, zeros))
+    for u in range(UNITS):
+        for slot, value in enumerate((f_y, fp_y)):
+            yrs[u, slot] = value[u]
+
+    def send_yr(t):
+        to = peer_y(t)
+        copy_y(yrs.at[to], yrr.at[me_y], syr, to, to, me_y).start()
+
+    each(GY, send_yr)
+    yrr[me_y] = yrs[me_y]
     each(GY, arrive_a)
     for j in range(GY):
         part = ga[j]
@@ -566,6 +673,7 @@
             copy_x(xs.at[q, to], xr.at[q, me_x], xsem.at[q], to, to, me_x).wait_send()
             copy_x(vs.at[q, to], vr.at[q, me_x], vsem.at[q], to, to, me_x).wait_send()
         copy_x(p1s.at[to], p1r.at[me_x], s1, to, to, me_x).wait_send()
+        copy_x(pas, par.at[me_x], spa, to, to, me_x).wait_send()
 
     def drain_y(t):
         to = peer_y(t)
@@ -739,6 +847,15 @@
         block(CAP, 128),
         pltpu.VMEM((CAP, 128), jnp.int32),
         pltpu.SMEM((CAP, 128), jnp.int32),
+        pltpu.VMEM((CAP, 128), jnp.int32),
+        pltpu.SMEM((CAP, 128), jnp.int32),
+        block(WIRE, 128),
+        block(16, 128),
+        block(GX, 16, 128),
+        pltpu.VMEM((GX, 128, WIRE), BF16),
+        block(GX, 8, WIRE),
+        block(128, 128),
+        pltpu.VMEM((WIRE, WIRE), BF16),
         block(4 * PLANE, 128),
         block(4 * PLANE, 128),
         block(WIRE, 128),
@@ -777,8 +894,9 @@
         sems(GY),
         sems(GY),
         sems(GY),
+        sems(GX),
         pltpu.SemaphoreType.DMA((3,)),
-        pltpu.SemaphoreType.DMA,
+        pltpu.SemaphoreType.DMA((2,)),
     ]
     staged, currents_next = pl.pallas_call(
         kernel,

time: 66.3 us -> 62.9 us (0.949)
  Pallas kernels: 65.5 us -> 62.2 us
    pallas_call x1, Pallas kernels: 62.4 us -> 59.1 us  [local(): pl.pallas_call(kernel, out_shape=(pltpu.VMEM((4, GX, CX, 8, 128), F32), p...]
where the time goes in v3:
time: 62.9 us; the launch traced here: 62.8 us
  Pallas kernels  62.2 us (99%)
  between operations  0.64 us (1%)
    pallas_call x1, Pallas kernels, local(): pl.pallas_call(kernel, out_shape=(pltpu.VMEM((4, GX, CX, 8, 128), F32), p...  59.1 us
    pallas_call x1, Pallas kernels, local(): pl.pallas_call(deliver, out_shape=(jax.ShapeDtypeStruct((CX, CY, NZ), F32...  3.11 us

profile of v3, /device:TPU:1, one launch (start us, length us, event | category | flops | bytes accessed | tf_op | source)
XLA Modules:
  0.0 62.8 jit_solution(15897117480201350487)
XLA Ops:
  0.6 59.1 %shard_map.77 = (f32[4,16,16,8,128]{4,3,2,1,0:T(8,128)S(1)}, f32[4,128]{1,0:T(4,128)S(1)}) custom-call(f32[16,128,512]{2,1,0:T(8,128)} %field.1, f32[16,128,512]{2,1,0:T(8,128)} %conduct.1, s32[4,128]{1,0:T(4,128)} %bitcast.11, s32[1,128]{1,0:T(1,128)} %count_h.1, f32[4,128]{1,0:T(4,128)} %bitcast.12, bf16[512,512]{1,0:T(8,128)(2,1)} %bitcast.10), custom_call_target="tpu_custom_call" | custom-call | tf_op jit(solution)/shard_map/pallas_call | solution.py:901
  59.7 3.1 %shard_map.78 = (f32[16,128,512]{2,1,0:T(8,128)}, f32[4,128]{1,0:T(4,128)}) custom-call(f32[4,16,16,8,128]{4,3,2,1,0:T(8,128)S(1)} %get-tuple-element.6.staged, f32[4,128]{1,0:T(4,128)S(1)} %get-tuple-element.7.cur_in), custom_call_target="tpu_custom_call" | custom-call | tf_op jit(solution)/shard_map/pallas_call | solution.py:914

commit v4 on v3

--- a/solution.py
+++ b/solution.py
@@ -20,6 +20,7 @@
 PLANE = CY * CX
 UNITS = 8
 EARLY = 2
+AHEAD = 5
 
 
 def inverse(value):
@@ -40,7 +41,10 @@
     count_h,
     cur_h,
     coupling,
-    ob,
+    ht,
+    my,
+    ay,
+    ends,
     cur_out,
     fb,
     cb,
@@ -50,9 +54,6 @@
     xr,
     vs,
     vr,
-    ht,
-    my,
-    ay,
     cw,
     hot,
     bhl,
@@ -244,8 +245,8 @@
     pl.semaphore_wait(barrier, GX - 1 + GY - 1)
     each(EARLY, lambda t: send_x(0, order(t)), 0)
     each(GX, eliminate_and_send, EARLY)
-    for q in range(1, 3):
-        each(GX - 1, lambda t, q=q: send_x(q, order(t)), 0)
+    each(GX - 1, lambda t: send_x(1, order(t)), 0)
+    each(AHEAD, lambda t: send_x(2, order(t)), 0)
     for q in range(4):
         xr[q, me_x] = xs[q, me_x]
 
@@ -317,6 +318,7 @@
 
     each(GX - 1, send_pa, 0)
     par[me_x] = pas[...]
+    each(GX - 1, lambda t: send_x(2, order(t)), AHEAD)
     each(GX - 1, lambda t: send_x(3, order(t)), 0)
 
     cb2 = cb.reshape(4 * PLANE, 128)
@@ -330,17 +332,8 @@
     def at_y(y, u):
         return pl.ds(pl.multiple_of(u * (8 * CY) + y * 8, 8), 8)
 
-    row_16 = lax.broadcasted_iota(jnp.int32, (CX, 128), 0)
-
-    def build_hot(y):
-        rows = row_16 + y * CX
-        for k in range(CAP):
-            match = jnp.where(rows == place_r[k : k + 1, :], 1.0, 0.0)
-            hot[pl.ds(pl.multiple_of(y * CX, CX), CX), quarter(k)] = match.astype(BF16)
-
     def factor(y, state):
         a, g, gp = state
-        build_hot(y)
         after = ground_y(y + 1)
         a_new, g_new, gp_new = [], [], []
         for u in range(UNITS):
@@ -356,7 +349,6 @@
     ones = [jnp.ones((8, 128), F32) for _ in range(UNITS)]
     zeros = [jnp.zeros((8, 128), F32) for _ in range(UNITS)]
     a_y, g_y, gp_y = lax.fori_loop(0, CY - 1, factor, (ones, ground_y(0), zeros))
-    build_hot(CY - 1)
     for u in range(UNITS):
         for slot, value in enumerate((a_y, g_y, gp_y)):
             ycs[u, slot] = value[u]
@@ -480,9 +472,7 @@
         each(4, four, 0)
 
     reduce_x(0)
-    send_back(0)
     reduce_x(1)
-    send_back(1)
 
     def arrive_pa(t):
         frm = peer_x(t)
@@ -491,7 +481,6 @@
     each(GX, arrive_pa)
     each(GX, build_lines, 0)
     reduce_x(2)
-    send_back(2)
     gather_x((0, 1, 2), True)
     reduce_x(3)
     gather_x((3,), False)
@@ -516,7 +505,8 @@
 
     each(GX, send_1)
     p1r[me_x] = p1s[me_x]
-    send_back(3)
+    for q in range(4):
+        send_back(q)
 
     row_m = lax.broadcasted_iota(jnp.int32, (128, WIRE), 0)
     lane_m = lax.broadcasted_iota(jnp.int32, (128, WIRE), 1)
@@ -560,8 +550,6 @@
         each(GX, arrive)
         each(4, group, 0)
 
-    substitute(0)
-    substitute(1)
     each(GX, arrive_1)
     total = p1r[0]
     for i in range(1, GX):
@@ -579,6 +567,89 @@
 
     each(GY, send_2)
     p2r[me_y] = p2s[me_y]
+    def tree(terms):
+        while len(terms) > 1:
+            terms = [a + b for a, b in zip(terms[::2], terms[1::2])]
+        return terms[0]
+
+    def sum_up(q):
+        def rows(n, state):
+            new = []
+            for i, u in enumerate((2 * q, 2 * q + 1)):
+                values = [ht[at_y(n * 8 + step, u), :] for step in range(8)]
+                for slot, ref in enumerate((wv, wp)):
+                    terms = [value * ref[at_y(n * 8 + step, u), :] for step, value in enumerate(values)]
+                    new.append(state[2 * i + slot] + tree(terms))
+            return new
+
+        sums = lax.fori_loop(0, CY // 8, rows, zeros[:4])
+        for i, u in enumerate((2 * q, 2 * q + 1)):
+            yrs[u, 0] = sums[2 * i]
+            yrs[u, 1] = sums[2 * i + 1]
+
+    substitute(0)
+    sum_up(0)
+    substitute(1)
+    sum_up(1)
+    each(GY, arrive_2)
+    row = jnp.concatenate([p2r[2 * j, 0:1, :] + p2r[2 * j + 1, 0:1, :] for j in range(4)], axis=1)
+    new_row = 0.5 * cur_row + exact_dot(row, cw2[...], ((1,), (1,)))
+    for a in range(4):
+        ys[a : a + 1, :] = new_row[:, 128 * a : 128 * a + 128]
+
+    def send_a(t):
+        to = peer_y(t)
+        copy_y(ys, ga.at[me_y], sa, to, to, me_y).start()
+
+    def arrive_a(t):
+        frm = peer_y(t)
+        copy_y(ys, ga.at[frm], sa, frm, frm, frm).wait_recv()
+
+    each(GY, send_a)
+    ga[me_y] = ys[...]
+    for k in range(CAP):
+        cur_out[k : k + 1, :] = exact_dot(new_row, spread[k], ((1,), (1,)))
+    substitute(2)
+    sum_up(2)
+    substitute(3)
+    sum_up(3)
+    def send_yr(t):
+        to = peer_y(t)
+        copy_y(yrs.at[to], yrr.at[me_y], syr, to, to, me_y).start()
+
+    each(GY, send_yr)
+    yrr[me_y] = yrs[me_y]
+    each(GY, arrive_a)
+    for j in range(GY):
+        part = ga[j]
+        for a in range(4):
+            gat[a, j : j + 1, :] = part[a : a + 1, :]
+
+    def send_b(t):
+        to = peer_x(t)
+        copy_x(gat.at[to // 4], gb.at[me_x], sb, to, to, me_x).start()
+
+    def arrive_b(t):
+        frm = peer_x(t)
+        copy_x(gat.at[0], gb.at[frm], sb, frm, frm, frm).wait_recv()
+
+    each(GX, send_b)
+    gb[me_x] = gat[me_x // 4]
+    def drain_x(t):
+        to = peer_x(t)
+        for q in range(4):
+            copy_x(xs.at[q, to], xr.at[q, me_x], xsem.at[q], to, to, me_x).wait_send()
+            copy_x(vs.at[q, to], vr.at[q, me_x], vsem.at[q], to, to, me_x).wait_send()
+        copy_x(p1s.at[to], p1r.at[me_x], s1, to, to, me_x).wait_send()
+        copy_x(pas, par.at[me_x], spa, to, to, me_x).wait_send()
+
+    def drain_y(t):
+        to = peer_y(t)
+        copy_y(p2s.at[to], p2r.at[me_y], s2, to, to, me_y).wait_send()
+        copy_y(ycs.at[to], ycr.at[me_y], syc, to, to, me_y).wait_send()
+        copy_y(yrs.at[to], yrr.at[me_y], syr, to, to, me_y).wait_send()
+        copy_y(pks, pkr.at[me_y], spk, to, to, me_y).wait_send()
+
     def arrive_pk(t):
         frm = peer_y(t)
         copy_y(pks, pkr.at[frm], spk, frm, frm, frm).wait_recv()
@@ -611,77 +682,19 @@
         more = ycr[r + 1, 2] if r < GY - 1 else 1.0
         q_y = ycr[r, 1] + more + a * m * q_y
     yk[0, 0] = inverse(q_y)
-    substitute(2)
-    each(GY, arrive_2)
-    row = jnp.concatenate([p2r[2 * j, 0:1, :] + p2r[2 * j + 1, 0:1, :] for j in range(4)], axis=1)
-    new_row = 0.5 * cur_row + exact_dot(row, cw2[...], ((1,), (1,)))
-    for a in range(4):
-        ys[a : a + 1, :] = new_row[:, 128 * a : 128 * a + 128]
-
-    def send_a(t):
-        to = peer_y(t)
-        copy_y(ys, ga.at[me_y], sa, to, to, me_y).start()
-
-    def arrive_a(t):
-        frm = peer_y(t)
-        copy_y(ys, ga.at[frm], sa, frm, frm, frm).wait_recv()
-
-    each(GY, send_a)
-    ga[me_y] = ys[...]
-    for k in range(CAP):
-        cur_out[k : k + 1, :] = exact_dot(new_row, spread[k], ((1,), (1,)))
-    substitute(3)
-    def sum_up(y, state):
-        f, fp = state
-        f_new, fp_new = [], []
-        for u in range(UNITS):
-            fp_new.append(fp[u] + ay[at_y(y, u), :] * f[u])
-            f_new.append(ht[at_y(y + 1, u), :] + f[u] * my[at_y(y, u), :])
-        return f_new, fp_new
-
-    first = [ht[at_y(0, u), :] for u in range(UNITS)]
-    f_y, fp_y = lax.fori_loop(0, CY - 1, sum_up, (first, zeros))
-    for u in range(UNITS):
-        for slot, value in enumerate((f_y, fp_y)):
-            yrs[u, slot] = value[u]
-
-    def send_yr(t):
-        to = peer_y(t)
-        copy_y(yrs.at[to], yrr.at[me_y], syr, to, to, me_y).start()
-
-    each(GY, send_yr)
-    yrr[me_y] = yrs[me_y]
-    each(GY, arrive_a)
-    for j in range(GY):
-        part = ga[j]
-        for a in range(4):
-            gat[a, j : j + 1, :] = part[a : a + 1, :]
-
-    def send_b(t):
-        to = peer_x(t)
-        copy_x(gat.at[to // 4], gb.at[me_x], sb, to, to, me_x).start()
-
-    def arrive_b(t):
-        frm = peer_x(t)
-        copy_x(gat.at[0], gb.at[frm], sb, frm, frm, frm).wait_recv()
-
-    each(GX, send_b)
-    gb[me_x] = gat[me_x // 4]
-    def drain_x(t):
-        to = peer_x(t)
-        for q in range(4):
-            copy_x(xs.at[q, to], xr.at[q, me_x], xsem.at[q], to, to, me_x).wait_send()
-            copy_x(vs.at[q, to], vr.at[q, me_x], vsem.at[q], to, to, me_x).wait_send()
-        copy_x(p1s.at[to], p1r.at[me_x], s1, to, to, me_x).wait_send()
-        copy_x(pas, par.at[me_x], spa, to, to, me_x).wait_send()
-
-    def drain_y(t):
-        to = peer_y(t)
-        copy_y(p2s.at[to], p2r.at[me_y], s2, to, to, me_y).wait_send()
-        copy_y(ycs.at[to], ycr.at[me_y], syc, to, to, me_y).wait_send()
-        copy_y(yrs.at[to], yrr.at[me_y], syr, to, to, me_y).wait_send()
-        copy_y(pks, pkr.at[me_y], spk, to, to, me_y).wait_send()
-
+    row_16 = lax.broadcasted_iota(jnp.int32, (CX, 128), 0)
+
+    def build_hot(y):
+        rows = row_16 + y * CX
+        for k in range(CAP):
+            match = jnp.where(rows == place_r[k : k + 1, :], 1.0, 0.0)
+            hot[pl.ds(pl.multiple_of(y * CX, CX), CX), quarter(k)] = match.astype(BF16)
+
+    def build_some(n):
+        for step in range(8):
+            build_hot(n * 8 + step)
+
+    each(CY // 8, build_some, 0)
     each(GX, drain_x)
     each(GY, drain_y)
     each(GX, arrive_b)
@@ -766,25 +779,7 @@
     lax.fori_loop(0, CY // 32, forward_y, zeros)
     each(GY, arrive_yv)
 
-    west_y = [yvr[u, 0] for u in range(UNITS)]
-    east_y = [yvr[u, 1] for u in range(UNITS)]
-    ob2 = ob.reshape(4 * PLANE, 128)
-
-    def finish(n, value):
-        c = CY // 8 - 1 - n
-        for back_step in range(8):
-            y = c * 8 + 7 - back_step
-            value = [
-                (ht[at_y(y, u), :] + ay[at_y(y, u), :] * west_y[u]) + my[at_y(y, u), :] * value[u]
-                for u in range(UNITS)
-            ]
-            for u in range(UNITS):
-                ob2[spread_rows(y, u), :] = value[u]
-        return value
-
-    for u in range(UNITS):
-        ht[at_y(CY - 1, u), :] = jnp.zeros((8, 128), F32)
-    lax.fori_loop(0, CY // 8, finish, east_y)
+    ends[...] = yvr[...]
 
     def drain_late_x(t):
         copy_x(gat.at[0], gb.at[me_x], sb, peer_x(t), peer_x(t), me_x).wait_send()
@@ -798,25 +793,56 @@
     each(GY, drain_late_y)
 
 
-def deliver(staged, cur_in, out, cur_out, sems):
-    def copy(d, q):
-        return pltpu.make_async_copy(
-            staged.at[q, d], out.at[:, pl.ds(pl.multiple_of(d * 8, 8), 8), 128 * q : 128 * q + 128], sems.at[q, d]
-        )
-
-    def start(d, carry):
-        for q in range(4):
-            copy(d, q).start()
+def deliver(ht, my, ay, ends, cur_in, out, cur_out, staged, sems):
+    rows = staged.reshape(4 * PLANE, 128)
+    west = [ends[u, 0] for u in range(UNITS)]
+    last = [ends[u, 1] for u in range(UNITS)]
+
+    def copies(c):
+        place = pl.ds(pl.multiple_of(c * 8, 8), 8)
+        return [
+            pltpu.make_async_copy(staged.at[q, c], out.at[:, place, 128 * q : 128 * q + 128], sems.at[q, c])
+            for q in range(4)
+        ]
+
+    def put(y, value):
+        for u in range(UNITS):
+            start = (u // 2) * PLANE + (y // 8) * (8 * CX) + (u % 2) * 64 + lax.rem(y, 8)
+            rows[pl.ds(start, 8, stride=8), :] = value[u]
+
+    def step(y, value):
+        new = []
+        for u in range(UNITS):
+            at = pl.ds(pl.multiple_of(u * (8 * CY) + y * 8, 8), 8)
+            new.append((ht[at, :] + ay[at, :] * west[u]) + my[at, :] * value[u])
+        put(y, new)
+        return new
+
+    def send(c):
+        for copy in copies(c):
+            copy.start()
+
+    def chunk(n, value):
+        c = CY // 8 - 1 - n
+        for back in range(8):
+            value = step(c * 8 + 7 - back, value)
+        send(c)
+        return value
+
+    put(CY - 1, last)
+    value = last
+    for back in range(1, 8):
+        value = step(CY - 1 - back, value)
+    send(CY // 8 - 1)
+    lax.fori_loop(1, CY // 8, chunk, value)
+    cur_out[...] = cur_in[...]
+
+    def wait(c, carry):
+        for copy in copies(c):
+            copy.wait()
         return carry
 
-    def wait(d, carry):
-        for q in range(4):
-            copy(d, q).wait()
-        return carry
-
-    lax.fori_loop(0, GX, start, 0)
-    cur_out[...] = cur_in[...]
-    lax.fori_loop(0, GX, wait, 0)
+    lax.fori_loop(0, CY // 8, wait, 0)
 
 
 def local(field, conduct, seg_cell, seg_count, currents, coupling):
@@ -834,9 +860,6 @@
         block(4, GX, 5, 8, 128),
         block(4, GX, 2, 8, 128),
         block(4, GX, 2, 8, 128),
-        block(4 * PLANE, 128),
-        block(4 * PLANE, 128),
-        block(4 * PLANE, 128),
         pltpu.VMEM((WIRE, WIRE), BF16),
         pltpu.VMEM((PLANE, WIRE), BF16),
         pltpu.VMEM((2 * WIRE, NZ), BF16),
@@ -898,17 +921,15 @@
         pltpu.SemaphoreType.DMA((3,)),
         pltpu.SemaphoreType.DMA((2,)),
     ]
-    staged, currents_next = pl.pallas_call(
+    rows = pltpu.VMEM((4 * PLANE, 128), F32)
+    *parts, currents_next = pl.pallas_call(
         kernel,
-        out_shape=(
-            pltpu.VMEM((4, GX, CX, 8, 128), F32),
-            pltpu.VMEM((CAP, 128), F32),
-        ),
+        out_shape=(rows, rows, rows, pltpu.VMEM((GY, 2, 8, 128), F32), pltpu.VMEM((CAP, 128), F32)),
         in_specs=[hbm] * 6,
-        out_specs=(vmem, vmem),
+        out_specs=(vmem,) * 5,
         scratch_shapes=scratch,
         compiler_params=pltpu.CompilerParams(
-            collective_id=0, has_side_effects=True, vmem_limit_bytes=57 * 1024 * 1024
+            collective_id=0, has_side_effects=True, vmem_limit_bytes=49 * 1024 * 1024
         ),
     )(field, conduct, cells, seg_count, currents[0].T, coupling[0])
     field_next, currents_next = pl.pallas_call(
@@ -917,11 +938,11 @@
             jax.ShapeDtypeStruct((CX, CY, NZ), F32),
             jax.ShapeDtypeStruct((CAP, 128), F32),
         ),
-        in_specs=[pl.BlockSpec(memory_space=pl.ANY), vmem],
+        in_specs=[vmem] * 5,
         out_specs=(hbm, vmem),
-        scratch_shapes=[pltpu.SemaphoreType.DMA((4, GX))],
-        compiler_params=pltpu.CompilerParams(vmem_limit_bytes=4 * 1024 * 1024),
-    )(staged, currents_next)
+        scratch_shapes=[block(4, GX, CX, 8, 128), pltpu.SemaphoreType.DMA((4, GX))],
+        compiler_params=pltpu.CompilerParams(vmem_limit_bytes=6 * 1024 * 1024),
+    )(*parts, currents_next)
     return field_next, currents_next.T[None]
 
 

time: 62.9 us -> 60.5 us (0.962)
  Pallas kernels: 62.2 us -> 59.7 us
    pallas_call x1, Pallas kernels: 59.1 us -> 56.2 us  [local(): pl.pallas_call(kernel, out_shape=(rows, rows, rows, pltpu.VMEM((GY, 2, 8,...]
where the time goes in v4:
time: 60.5 us; the launch traced here: 60.4 us
  Pallas kernels  59.7 us (99%)
  between operations  0.64 us (1%)
    pallas_call x1, Pallas kernels, local(): pl.pallas_call(kernel, out_shape=(rows, rows, rows, pltpu.VMEM((GY, 2, 8,...  56.2 us
    pallas_call x1, Pallas kernels, local(): pl.pallas_call(deliver, out_shape=(jax.ShapeDtypeStruct((CX, CY, NZ), F32...  3.5 us

profile of v4, /device:TPU:1, one launch (start us, length us, event | category | flops | bytes accessed | tf_op | source)
XLA Modules:
  0.0 60.4 jit_solution(222141962061185121)
XLA Ops:
  0.6 56.2 %shard_map.77 = (f32[8192,128]{1,0:T(8,128)S(1)}, f32[8192,128]{1,0:T(8,128)S(1)}, f32[8192,128]{1,0:T(8,128)S(1)}, f32[8,2,8,128]{3,2,1,0:T(8,128)S(1)}, f32[4,128]{1,0:T(4,128)S(1)}) custom-call(f32[16,128,512]{2,1,0:T(8,128)} %field.1, f32[16,128,512]{2,1,0:T(8,128)} %conduct.1, s32[4,128]{1,0:T(4,128)} %bitcast.11, s32[1,128]{1,0:T(1,128)} %count_h.1, ...), custom_call_target="tpu_custom_call" | custom-call | tf_op jit(solution)/shard_map/pallas_call | solution.py:925
  56.9 3.5 %shard_map.78 = (f32[16,128,512]{2,1,0:T(8,128)}, f32[4,128]{1,0:T(4,128)}) custom-call(f32[8192,128]{1,0:T(8,128)S(1)} %get-tuple-element.9.ht, f32[8192,128]{1,0:T(8,128)S(1)} %get-tuple-element.10.my, f32[8192,128]{1,0:T(8,128)S(1)} %get-tuple-element.11.ay, f32[8,2,8,128]{3,2,1,0:T(8,128)S(1)} %get-tuple-element.12.ends, ...), custom_call_target="tpu_custom_call" | custom-call | tf_op jit(solution)/shard_map/pallas_call | solution.py:935

commit v5 on v4

--- a/solution.py
+++ b/solution.py
@@ -151,7 +151,7 @@
 
     def order(t):
         u = 15 - t
-        return lax.rem(me_x // 4 + u // 4, 4) * 4 + lax.rem(me_x + lax.rem(u, 4), 4)
+        return lax.rem(me_x // 4 + lax.rem(u, 4), 4) * 4 + lax.rem(me_x + u // 4 + u, 4)
 
     def start_in(t, carry):
         for copy in in_copies(order(t)):
@@ -589,8 +589,6 @@
 
     substitute(0)
     sum_up(0)
-    substitute(1)
-    sum_up(1)
     each(GY, arrive_2)
     row = jnp.concatenate([p2r[2 * j, 0:1, :] + p2r[2 * j + 1, 0:1, :] for j in range(4)], axis=1)
     new_row = 0.5 * cur_row + exact_dot(row, cw2[...], ((1,), (1,)))
@@ -609,6 +607,8 @@
     ga[me_y] = ys[...]
     for k in range(CAP):
         cur_out[k : k + 1, :] = exact_dot(new_row, spread[k], ((1,), (1,)))
+    substitute(1)
+    sum_up(1)
     substitute(2)
     sum_up(2)
     substitute(3)

time: 60.5 us -> 59.9 us (0.990)
  no operation moved by 1% of the time
where the time goes in v5:
time: 59.9 us; the launch traced here: 59.8 us
  Pallas kernels  59.2 us (99%)
  between operations  0.64 us (1%)
    pallas_call x1, Pallas kernels, local(): pl.pallas_call(kernel, out_shape=(rows, rows, rows, pltpu.VMEM((GY, 2, 8,...  55.7 us
    pallas_call x1, Pallas kernels, local(): pl.pallas_call(deliver, out_shape=(jax.ShapeDtypeStruct((CX, CY, NZ), F32...  3.5 us

profile of v5, /device:TPU:1, one launch (start us, length us, event | category | flops | bytes accessed | tf_op | source)
XLA Modules:
  0.0 59.8 jit_solution(13809802873497766174)
XLA Ops:
  0.6 55.7 %shard_map.77 = (f32[8192,128]{1,0:T(8,128)S(1)}, f32[8192,128]{1,0:T(8,128)S(1)}, f32[8192,128]{1,0:T(8,128)S(1)}, f32[8,2,8,128]{3,2,1,0:T(8,128)S(1)}, f32[4,128]{1,0:T(4,128)S(1)}) custom-call(f32[16,128,512]{2,1,0:T(8,128)} %field.1, f32[16,128,512]{2,1,0:T(8,128)} %conduct.1, s32[4,128]{1,0:T(4,128)} %bitcast.11, s32[1,128]{1,0:T(1,128)} %count_h.1, ...), custom_call_target="tpu_custom_call" | custom-call | tf_op jit(solution)/shard_map/pallas_call | solution.py:925
  56.3 3.5 %shard_map.78 = (f32[16,128,512]{2,1,0:T(8,128)}, f32[4,128]{1,0:T(4,128)}) custom-call(f32[8192,128]{1,0:T(8,128)S(1)} %get-tuple-element.9.ht, f32[8192,128]{1,0:T(8,128)S(1)} %get-tuple-element.10.my, f32[8192,128]{1,0:T(8,128)S(1)} %get-tuple-element.11.ay, f32[8,2,8,128]{3,2,1,0:T(8,128)S(1)} %get-tuple-element.12.ends, ...), custom_call_target="tpu_custom_call" | custom-call | tf_op jit(solution)/shard_map/pallas_call | solution.py:935

commit v6 on v5

--- a/solution.py
+++ b/solution.py
@@ -21,6 +21,7 @@
 UNITS = 8
 EARLY = 2
 AHEAD = 5
+SENT = 3 * CAP
 
 
 def inverse(value):
@@ -306,15 +307,15 @@
     for k in range(CAP):
         hit = hit_of(k)
         rows = slice(128 * k, 128 * k + 128)
-        for slot, ref in enumerate((samp, samp2, samp3)):
+        for slot, ref in ((3, samp), (0, samp2), (1, samp3)):
             chosen = jnp.where(hit, ref[rows, :], 0.0) * KY
             pas[slot * CAP + k : slot * CAP + k + 1, :] = jnp.sum(chosen.T, axis=0, keepdims=True)
     key = ((cells >> 12) & 15) * 32 + ((cells >> 7) & 3) * 8 + ((cells >> 9) & 7)
-    pas[3 * CAP : 4 * CAP, :] = (key * 128 + (cells & 127)).astype(F32)
+    pas[2 * CAP : 3 * CAP, :] = (key * 128 + (cells & 127)).astype(F32)
 
     def send_pa(t):
         to = order(t)
-        copy_x(pas, par.at[me_x], spa, to, to, me_x).start()
+        copy_x(pas.at[0:SENT], par.at[me_x, 0:SENT], spa, to, to, me_x).start()
 
     each(GX - 1, send_pa, 0)
     par[me_x] = pas[...]
@@ -437,15 +438,15 @@
     row_128 = lax.broadcasted_iota(jnp.int32, (128, 128), 0)
 
     def build_lines(r):
-        code = par[r, 3 * CAP : 4 * CAP, :].astype(jnp.int32)
+        code = par[r, 2 * CAP : SENT, :].astype(jnp.int32)
         for k in range(CAP):
             match = jnp.where(row_128 == (code[k : k + 1, :] & 127), 1.0, 0.0)
             lines[r, :, quarter(k)] = match.astype(BF16)
 
     def gather_x(quarters, first):
         def one(r):
-            info = par[r]
-            code = info[3 * CAP : 4 * CAP, :].astype(jnp.int32)
+            info = par[r, 0 : 2 * CAP, :]
+            code = par[r, 2 * CAP : SENT, :].astype(jnp.int32)
             parts = []
             for q in quarters:
                 value = vs[q, r].reshape(16, 128)
@@ -458,25 +459,23 @@
                     solved = product[32 * n : 32 * n + 16, quarter(k)] + product[32 * n + 16 : 32 * n + 32, quarter(k)]
                     match = (code[k : k + 1, :] >> 7) == me_x * 32 + q * 8 + row_8
                     value = (
-                        info[k : k + 1, :]
-                        + info[CAP + k : CAP + k + 1, :] * solved[0:8]
-                        + info[2 * CAP + k : 2 * CAP + k + 1, :] * solved[8:16]
+                        info[k : k + 1, :] * solved[0:8] + info[CAP + k : CAP + k + 1, :] * solved[8:16]
                     )
                     total = total + jnp.where(match, value, 0.0)
                 acc[r, :, quarter(k)] = total
 
-        def four(n):
-            for i in range(4):
-                one(n * 4 + i)
-
-        each(4, four, 0)
+        def eight(n):
+            for i in range(8):
+                one(n * 8 + i)
+
+        each(2, eight, 0)
 
     reduce_x(0)
     reduce_x(1)
 
     def arrive_pa(t):
         frm = peer_x(t)
-        copy_x(pas, par.at[frm], spa, frm, frm, frm).wait_recv()
+        copy_x(pas.at[0:SENT], par.at[frm, 0:SENT], spa, frm, frm, frm).wait_recv()
 
     each(GX, arrive_pa)
     each(GX, build_lines, 0)
@@ -492,7 +491,8 @@
     for r in range(GX):
         total = jnp.sum(acc[r], axis=0, keepdims=True)
         for k in range(CAP):
-            tmat[pl.ds(lax.rem(me_y, 2) * 64 + CAP * r + k, 1), :] = total[:, quarter(k)]
+            own = jnp.where(me_x == r, pas[3 * CAP + k : 3 * CAP + k + 1, :], 0.0)
+            tmat[pl.ds(lax.rem(me_y, 2) * 64 + CAP * r + k, 1), :] = total[:, quarter(k)] + own
     p1s[...] = tmat[...].T.reshape(GX, GY, 128)
 
     def send_1(t):
@@ -641,7 +641,7 @@
             copy_x(xs.at[q, to], xr.at[q, me_x], xsem.at[q], to, to, me_x).wait_send()
             copy_x(vs.at[q, to], vr.at[q, me_x], vsem.at[q], to, to, me_x).wait_send()
         copy_x(p1s.at[to], p1r.at[me_x], s1, to, to, me_x).wait_send()
-        copy_x(pas, par.at[me_x], spa, to, to, me_x).wait_send()
+        copy_x(pas.at[0:SENT], par.at[me_x, 0:SENT], spa, to, to, me_x).wait_send()
 
     def drain_y(t):
         to = peer_y(t)

time: 59.9 us -> 59.4 us (level)
  Pallas kernels: 59.2 us -> 58.6 us
where the time goes in v6:
time: 59.4 us; the launch traced here: 59.2 us
  Pallas kernels  58.6 us (99%)
  between operations  0.64 us (1%)
    pallas_call x1, Pallas kernels, local(): pl.pallas_call(kernel, out_shape=(rows, rows, rows, pltpu.VMEM((GY, 2, 8,...  55.1 us
    pallas_call x1, Pallas kernels, local(): pl.pallas_call(deliver, out_shape=(jax.ShapeDtypeStruct((CX, CY, NZ), F32...  3.5 us

profile of v6, /device:TPU:1, one launch (start us, length us, event | category | flops | bytes accessed | tf_op | source)
XLA Modules:
  0.0 59.2 jit_solution(2895013968508271462)
XLA Ops:
  0.6 55.1 %shard_map.77 = (f32[8192,128]{1,0:T(8,128)S(1)}, f32[8192,128]{1,0:T(8,128)S(1)}, f32[8192,128]{1,0:T(8,128)S(1)}, f32[8,2,8,128]{3,2,1,0:T(8,128)S(1)}, f32[4,128]{1,0:T(4,128)S(1)}) custom-call(f32[16,128,512]{2,1,0:T(8,128)} %field.1, f32[16,128,512]{2,1,0:T(8,128)} %conduct.1, s32[4,128]{1,0:T(4,128)} %bitcast.11, s32[1,128]{1,0:T(1,128)} %count_h.1, ...), custom_call_target="tpu_custom_call" | custom-call | tf_op jit(solution)/shard_map/pallas_call | solution.py:925
  55.7 3.5 %shard_map.78 = (f32[16,128,512]{2,1,0:T(8,128)}, f32[4,128]{1,0:T(4,128)}) custom-call(f32[8192,128]{1,0:T(8,128)S(1)} %get-tuple-element.9.ht, f32[8192,128]{1,0:T(8,128)S(1)} %get-tuple-element.10.my, f32[8192,128]{1,0:T(8,128)S(1)} %get-tuple-element.11.ay, f32[8,2,8,128]{3,2,1,0:T(8,128)S(1)} %get-tuple-element.12.ends, ...), custom_call_target="tpu_custom_call" | custom-call | tf_op jit(solution)/shard_map/pallas_call | solution.py:935
